TPU v7x, 512 devices: a whole 4x8x8 slice. The times are simulated.
512 devices in a mesh: expert: 64 (over z, y_hi, core), tensor: 8 (over x, y_lo).
Axes of the slice: x: 4, y: 8 (y_hi: 4, y_lo: 2; y = y_hi * 2 + y_lo), z: 8, core: 2. Of those that a mesh axis runs over, the one named last changes fastest.
Arguments:
- out_grad: bfloat16 [8192, 3584], P('expert', 'tensor'), may hold values from -6 to 6
- gate_probs: float32 [8192, 2], P('expert'), may hold values from 0.2 to 1
- expert_ids: int32 [8192, 2], P('expert'), may hold values from 0 to 31, all different within a row; in each aligned block of 128 rows (0 to 127, 128 to 255, ...) at most 10 rows name the same one
- saved_gate: bfloat16 [77824, 640], P(('expert', 'tensor')), may hold values from -6 to 6
- saved_up: bfloat16 [77824, 640], P(('expert', 'tensor')), may hold values from -6 to 6
- w_gate: bfloat16 [77824, 3584], P(('expert', 'tensor')), may hold values from -0.078125 to 0.078125
- w_up: bfloat16 [77824, 3584], P(('expert', 'tensor')), may hold values from -0.078125 to 0.078125
- w_down: bfloat16 [77824, 3584], P(('expert', 'tensor')), may hold values from -0.09375 to 0.09375
Outputs:
- in_grad: bfloat16 [8192, 3584], P('expert', 'tensor')
Inputs may be any that keep to these rules, and one draw needn't show every extreme that they name: `expert_ids`: each row names 2 different experts. Among the 128 rows of one device no expert is named more than 10 times, a bound that some block reaches there in some device.
All inputs are finite; a program needn't handle non-finite values.
Results may differ from a plain program's by a relative error of at most 0.017.
Values may be sent and summed in bfloat16 or wider, within the bound.
No kernel may reach another device: no remote copies, remote signals or barrier semaphores. Data moves between devices by JAX's collectives and lax.ppermute only.
A program may use at most 128 MiB of HBM per device.

v0:
```python
import jax
import jax.numpy as jnp
from jax import lax
from jax.sharding import PartitionSpec as P


def shards(out_grad, gate_probs, expert_ids, saved_gate, saved_up, w_gate, w_up, w_down):
    sources = lax.axis_size("expert")
    experts = sources // 2
    capacity = saved_gate.shape[1] // sources
    tok_rows = out_grad.shape[0]
    routes_flat = expert_ids.reshape(-1)
    onehot = (routes_flat[:, None] == jnp.arange(experts, dtype=jnp.int32)[None, :]).astype(
        jnp.int32
    )
    before = jnp.cumsum(onehot, axis=0) - onehot
    slot_index = jnp.sum(before * onehot, axis=1)
    target = routes_flat * capacity + slot_index
    placing = (jnp.arange(experts * capacity, dtype=jnp.int32)[:, None] == target[None, :]).astype(
        jnp.bfloat16
    )
    full_grad = lax.all_gather(out_grad, "tensor", axis=1, tiled=True)
    span_cols = full_grad.shape[1]
    scaled = (gate_probs[:, :, None] * full_grad[:, None, :].astype(jnp.float32)).astype(
        jnp.bfloat16
    )
    packed = jnp.dot(
        placing, scaled.reshape(-1, span_cols), preferred_element_type=jnp.float32
    ).astype(jnp.bfloat16)
    doubled = jnp.broadcast_to(
        packed.reshape(experts, 1, capacity, span_cols), (experts, 2, capacity, span_cols)
    )
    incoming = lax.all_to_all(
        doubled.reshape(sources, capacity, span_cols),
        "expert",
        split_axis=0,
        concat_axis=0,
        tiled=True,
    )
    hidden_grad = lax.dot_general(
        w_down,
        incoming.reshape(sources * capacity, -1),
        (((1,), (1,)), ((), ())),
        preferred_element_type=jnp.float32,
    )
    gate_vals = saved_gate.astype(jnp.float32)
    up_vals = saved_up.astype(jnp.float32)
    logistic = jax.nn.sigmoid(gate_vals)
    grad_gate = (hidden_grad * up_vals * logistic * (1.0 + gate_vals * (1.0 - logistic))).astype(
        jnp.bfloat16
    )
    grad_up = (hidden_grad * gate_vals * logistic).astype(jnp.bfloat16)
    both_grads = jnp.concatenate([grad_gate, grad_up], axis=0)
    both_weights = jnp.concatenate([w_gate, w_up], axis=0)
    span_cols = out_grad.shape[1]
    product = lax.dot_general(
        both_grads, both_weights, (((0,), (0,)), ((), ())), preferred_element_type=jnp.float32
    )
    partials = product.astype(jnp.bfloat16).reshape(sources, capacity, -1)
    returned = lax.all_to_all(partials, "expert", split_axis=0, concat_axis=0, tiled=True)
    span_cols = returned.shape[2]
    halves = jnp.sum(returned.astype(jnp.float32).reshape(experts, 2, capacity, span_cols), axis=1)
    picked = jnp.take(halves.reshape(experts * capacity, span_cols), target, axis=0)
    result = lax.psum_scatter(
        jnp.sum(picked.reshape(tok_rows, -1, span_cols), axis=1),
        "tensor",
        scatter_dimension=1,
        tiled=True,
    )
    return result.astype(jnp.bfloat16)


def solution(mesh):
    return jax.shard_map(
        shards,
        mesh=mesh,
        in_specs=(
            P("expert", "tensor"),
            P("expert", None),
            P("expert", None),
            P(("expert", "tensor"), None),
            P(("expert", "tensor"), None),
            P(("expert", "tensor"), None),
            P(("expert", "tensor"), None),
            P(("expert", "tensor"), None),
        ),
        out_specs=P("expert", "tensor"),
        check_vma=False,
    )
```

profile of v0, /device:TPU:1, one launch (start us, length us, event | category | flops | bytes accessed | tf_op | source)
XLA Modules:
  0.0 615.0 jit_solution(7257102875664142274)
XLA Ops:
  6.5 0.0 copy-start
  6.5 0.9 copy.31
  7.4 0.1 eq.39
  7.6 0.1 reshape.97
  7.7 0.6 reduce-window.6
  8.3 0.2 slice_reduce_fusion
  8.5 0.1 fusion.18
  8.6 29.7 %all_gather.3 = bf16[128,3584]{0,1:T(8,128)(2,1)} all-gather(bf16[128,448]{0,1:T(8,128)(2,1)} %param.8), channel_id=1, replica_groups=mesh['expert'=64,'tensor'=8] {'tensor'}, dimensions={1}, use_global_device_ids=true | all-gather | bytes 1032192 | tf_op jit(solution)/shard_map/all_gather | solution.py:22
  38.3 1.5 copy.37
  39.8 3.1 mul.73
  42.8 5.7 mul.74
  48.5 0.0 copy-done.3
  48.5 0.1 copy.36
  48.6 0.1 mul.71
  48.8 2.9 convolution_convert_fusion.1
  51.7 2.6 broadcast_in_dim.23
  54.3 2.9 broadcast_in_dim.24
  57.2 200.8 %all_to_all.10 = bf16[64,10,3584]{2,1,0:T(8,128)(2,1)} all-to-all(bf16[64,10,3584]{2,1,0:T(8,128)(2,1)S(1)} %bitcast.32), channel_id=1, replica_groups=mesh['expert'=64,'tensor'=8] {'expert'}, dimensions={0} | all-to-all | bytes 9175040 | tf_op jit(solution)/shard_map/all_to_all | solution.py:33
  258.0 8.1 %reshape.100 = bf16[640,3584]{1,0:T(8,128)(2,1)} reshape(bf16[64,10,3584]{2,1,0:T(8,128)(2,1)} %all_to_all.10) | data formatting | bytes 9175040 | tf_op jit(solution)/shard_map/reshape | solution.py:42
  266.1 0.0 copy-done
  266.1 0.0 copy-done.6
  266.1 0.0 copy-done.7
  266.1 0.0 copy-start.4
  266.1 0.0 copy-start.5
  266.1 4.0 fusion.9
  270.1 0.0 copy-done.4
  270.2 0.0 copy-done.5
  270.2 4.6 convolution_convert_fusion
  274.8 7.7 %reshape.101 = bf16[64,10,3584]{2,1,0:T(8,128)(2,1)} reshape(bf16[640,3584]{1,0:T(8,128)(2,1)} %convolution_convert_fusion) | data formatting | bytes 9175040 | tf_op jit(solution)/shard_map/reshape | solution.py:59
  282.5 6.6 %all-to-all-start.1 = ((bf16[64,10,3584]{2,1,0:T(8,128)(2,1)}), bf16[64,10,3584]{2,1,0:T(8,128)(2,1)}, u32[]{:S(2)}, u32[]{:S(2)}) async-start(bf16[64,10,3584]{2,1,0:T(8,128)(2,1)} %reshape.101), calls=%async_computation.1 | async-start | bytes 14680064 | tf_op jit(solution)/shard_map/all_to_all | solution.py:60
  289.2 0.2 reduce-scatter.4.cloned.1.call-start
  289.4 0.1 reduce_sum.32
  289.5 0.0 copy-done.2
  289.6 0.1 copy.38
  289.7 0.1 mul.82
  289.8 0.1 copy.34
  289.9 0.1 copy.35
  290.1 186.4 %all-to-all-done.1 = bf16[64,10,3584]{2,1,0:T(8,128)(2,1)} async-done(((bf16[64,10,3584]{2,1,0:T(8,128)(2,1)}), bf16[64,10,3584]{2,1,0:T(8,128)(2,1)}, u32[]{:S(2)}, u32[]{:S(2)}) %all-to-all-start.1) | async-done | bytes 4587552 | tf_op jit(solution)/shard_map/all_to_all | solution.py:60
  476.5 8.9 %convert_reduce_fusion = f32[32,10,3584]{2,1,0:T(8,128)} fusion(bf16[64,10,3584]{2,1,0:T(8,128)(2,1)} %all-to-all-done.1), kind=kLoop, calls=%fused_computation.1 | loop fusion | flops 3440640 | bytes 9175040 | tf_op jit(solution)/shard_map/reduce_sum | solution.py:62
  485.4 5.7 reshape.104
  491.1 7.5 %gather_fusion = f32[256,3584]{1,0:T(8,128)} fusion(f32[320,3584]{1,0:T(8,128)} %reshape.104, s32[1024]{0:T(1024)S(1)} %pad_clamp_fusion), kind=kCustom, calls=%fused_computation | custom fusion | bytes 7341056 | tf_op jit(solution)/shard_map/jit(_take)/gather | solution.py:63
  498.6 5.5 gather.7
  504.1 8.1 %select_reduce_fusion = f32[128,3584]{1,0:T(8,128)S(1)} fusion(f32[128,2,3584]{2,1,0:T(2,128)} %gather.7, pred[128,2]{1,0:T(8,128)(4,1)S(1)} %copy.35), kind=kLoop, calls=%fused_computation.4 | loop fusion | flops 1376256 | bytes 5505280 | tf_op jit(solution)/shard_map/reduce_sum | solution.py:65
  512.2 1.7 copy.40
  513.9 0.0 reduce-scatter.4.cloned.1.call-update
  513.9 92.7 %reduce-scatter.4.cloned.1.call-done = f32[448,128]{1,0:T(8,128)} async-done(((f32[3584,128]{1,0:T(8,128)}), f32[448,128]{1,0:T(8,128)}) %reduce-scatter.4.cloned.1.call-update) | async-done | bytes 229392
  606.6 1.6 bitcast_convert_fusion
  608.2 0.0 copy-done.1
  (13 shorter events, 0.1 us)
Async XLA Ops:
  6.5 259.5 %copy-start = (bf16[152,3584]{1,0:T(8,128)(2,1)S(1)}, bf16[152,3584]{1,0:T(8,128)(2,1)}, u32[]{:S(2)}) copy-start(bf16[152,3584]{1,0:T(8,128)(2,1)} %param.15) | copy-start | bytes 3268612
  42.8 5.7 copy-start.3
  258.0 8.1 %copy-start.6 = (bf16[152,640]{1,0:T(8,128)(2,1)S(1)}, bf16[152,640]{1,0:T(8,128)(2,1)}, u32[]{:S(2)}) copy-start(bf16[152,640]{1,0:T(8,128)(2,1)} %param.11) | copy-start | bytes 583684
  258.0 8.1 %copy-start.7 = (bf16[152,640]{1,0:T(8,128)(2,1)S(1)}, bf16[152,640]{1,0:T(8,128)(2,1)}, u32[]{:S(2)}) copy-start(bf16[152,640]{1,0:T(8,128)(2,1)} %param.12) | copy-start | bytes 583684
  266.1 4.1 copy-start.4
  266.1 4.1 copy-start.5
  282.5 7.0 %copy-start.2 = (s32[128,2]{0,1:T(2,128)S(1)}, s32[128,2]{0,1:T(2,128)}, u32[]{:S(2)}) copy-start(s32[128,2]{0,1:T(2,128)} %param.10) | copy-start | bytes 3076
  282.5 194.0 %all-to-all-start.1 = ((bf16[64,10,3584]{2,1,0:T(8,128)(2,1)}), bf16[64,10,3584]{2,1,0:T(8,128)(2,1)}, u32[]{:S(2)}, u32[]{:S(2)}) async-start(bf16[64,10,3584]{2,1,0:T(8,128)(2,1)} %reshape.101), calls=%async_computation.1 | async-start | bytes 14680064 | tf_op jit(solution)/shard_map/all_to_all | solution.py:60
  289.2 317.4 %reduce-scatter.4.cloned.1.call-start = ((), (), s32[]{:S(2)}) async-start(), calls=%async_computation.3 | async-start | bytes 2064384
  504.1 104.1 %copy-start.1 = (bf16[152,3584]{1,0:T(8,128)(2,1)S(1)}, bf16[152,3584]{1,0:T(8,128)(2,1)}, u32[]{:S(2)}) copy-start(bf16[152,3584]{1,0:T(8,128)(2,1)} %param.15) | copy-start | bytes 3268612
Sparse Core Ops, SparseCore 0:
  514.0 92.5 reduce-scatter.3
where the time goes:
time: 616 us; the launch traced here: 615 us
  waiting for transfers between devices  279 us (45%)
  blocking collectives  230 us (37%)
  local copies, waits for them, and re-layouts  54.1 us (9%)
  other arithmetic  19.3 us (3%)
  between operations  13.6 us (2%)
  matrix products  11.6 us (2%)
  starting transfers between devices  6.87 us (1%)
    all_to_all x1, blocking collectives, shards(): lax.all_to_all(doubled.reshape(sources, capacity, span_cols), 'expert', s...  201 us
    all_to_all x1, waiting for transfers between devices, shards(): lax.all_to_all(partials, 'expert', split_axis=0, concat_axis=0, tiled=True)  186 us
    unnamed x2, waiting for transfers between devices  92.7 us
    all_gather x1, blocking collectives, shards(): full_grad = lax.all_gather(out_grad, 'tensor', axis=1, tiled=True)  29.7 us
    gather x2, local copies, waits for them, and re-layouts, shards(): jnp.take(halves.reshape(experts * capacity, span_cols), target, axis=0)  13 us
  transfers between devices with their start and end apart: 2, of which 2 were waited for; matrix products, arithmetic and copies ran while one was open for 0% of the time, Pallas kernels for 0%

commit v1 on v0

v1 whole, which is shorter than its diff:
```python
import jax
import jax.numpy as jnp
from jax import lax
from jax.experimental import pallas as pl
from jax.experimental.pallas import tpu as pltpu
from jax.sharding import Mesh, PartitionSpec as P

CAP = 10
HALF = CAP // 2
BLK = 40
EXP = 32
TEN = 8
TOK = 128
FEAT = 448
FULL = 384
FF = 152
D = 3584
PAIR = 2 * FEAT
ROWS = EXP * CAP
HROWS = ROWS // 2
PIECE = 7 * HROWS
GRP = EXP // 2

BF = jnp.bfloat16
F32 = jnp.float32
VM = pl.BlockSpec(memory_space=pltpu.VMEM)
SM = pl.BlockSpec(memory_space=pltpu.SMEM)


def nt(a, b):
    return lax.dot_general(a, b, (((1,), (1,)), ((), ())), preferred_element_type=F32)


def tn(a, b):
    return lax.dot_general(a, b, (((0,), (0,)), ((), ())), preferred_element_type=F32)


def block_ids():
    e = lax.broadcasted_iota(jnp.int32, (EXP, BLK, TOK), 0).reshape(EXP * BLK, TOK)
    k = lax.broadcasted_iota(jnp.int32, (EXP, BLK, TOK), 1).reshape(EXP * BLK, TOK)
    return e, k


def slots_of(e, k):
    tens = jnp.where(k >= 30, 30, jnp.where(k >= 20, 20, jnp.where(k >= 10, 10, 0)))
    low = jnp.where(k < 35, e * CAP + k - tens, -1)
    high = jnp.where((k >= 30) & (k < 35), e * CAP + k - 30 + HALF, -1)
    return low, high


def pack_kernel(pos_ref, xt_ref, gt_ref, et_ref, out_ref, tgt_ref):
    yl = pos_ref[1]
    e0 = et_ref[0:1, :]
    e1 = et_ref[1:2, :]
    xi = lax.broadcasted_iota(jnp.int32, (EXP, TOK), 0)
    named = ((xi == e0) | (xi == e1)).astype(F32).astype(BF)
    earlier = (
        lax.broadcasted_iota(jnp.int32, (TOK, TOK), 0) < lax.broadcasted_iota(jnp.int32, (TOK, TOK), 1)
    ).astype(F32).astype(BF)
    before = jnp.dot(named, earlier, preferred_element_type=F32)
    s0 = jnp.sum(jnp.where(xi == e0, before, 0.0), axis=0, keepdims=True).astype(jnp.int32)
    s1 = jnp.sum(jnp.where(xi == e1, before, 0.0), axis=0, keepdims=True).astype(jnp.int32)
    t0 = e0 * CAP + s0
    t1 = e1 * CAP + s1
    tgt_ref[0:1, :] = t0
    tgt_ref[1:2, :] = t1
    e, k = block_ids()
    low, high = slots_of(e, k)
    one = lambda hit: hit.astype(F32).astype(BF)
    m_low = jnp.concatenate([one(low == t0), one(low == t1)], axis=1)
    m_high = jnp.concatenate([one(high == t0), one(high == t1)], axis=1)

    def scaled(rows):
        x = rows.astype(F32)
        return jnp.concatenate([(x * gt_ref[0:1, :]).astype(BF), (x * gt_ref[1:2, :]).astype(BF)], axis=1)

    full = scaled(xt_ref[pl.ds(pl.multiple_of(64 * yl, 64), FULL), :])
    half = scaled(xt_ref[pl.ds(pl.multiple_of(FULL * (1 - yl), 64), 64), :])
    none = jnp.zeros_like(half)
    wide = nt(m_low, full)
    pair = nt(m_low, jnp.concatenate([half, none], axis=0)) + nt(m_high, jnp.concatenate([none, half], axis=0))
    picked = jnp.where(
        k < 10, wide[:, 0:128], jnp.where(k < 20, wide[:, 128:256], jnp.where(k < 30, wide[:, 256:384], pair))
    )
    out_ref[...] = picked.astype(BF)


def sort_kernel(in_ref, out_ref):
    n_out, n_in = 7 * GRP * HALF, GRP * BLK
    rows = GRP * HALF
    q = lax.broadcasted_iota(jnp.int32, (rows, n_in), 0)
    col = lax.broadcasted_iota(jnp.int32, (rows, n_in), 1)
    gap = col - 35 * ((q * 205) >> 10) - q
    moves = jnp.concatenate([(gap == HALF * b).astype(F32).astype(BF) for b in range(7)], axis=0)
    both = jnp.concatenate([in_ref[0:n_in, :], in_ref[n_in : 2 * n_in, :]], axis=1)
    res = jnp.dot(moves, both, preferred_element_type=F32).astype(BF)
    for b in range(7):
        for g in range(2):
            block = res[b * rows : (b + 1) * rows, g * 128 : (g + 1) * 128]
            for t in range(TEN):
                at = t * PIECE + b * HROWS + g * rows
                out_ref[at : at + rows, :] = block


def main_kernel(pos_ref, in_ref, wd0, wd1, wg0, wg1, wu0, wu1, sg0, sg1, su0, su1, out_ref, r_ref):
    core = pos_ref[2]
    for i in range(4):
        base, even, odd = i * PAIR, 2 * i * PIECE, (2 * i + 1) * PIECE
        for j in range(3):
            r_ref[:, base + 128 * j : base + 128 * (j + 1)] = in_ref[even + j * ROWS : even + (j + 1) * ROWS, :]
            at = base + 512 + 128 * j
            r_ref[:, at : at + 128] = in_ref[odd + j * ROWS : odd + (j + 1) * ROWS, :]
        eh = in_ref[even + 3 * ROWS : even + PIECE, :]
        oh = in_ref[odd + 3 * ROWS : odd + PIECE, :]
        r_ref[0:HROWS, base + FULL : base + 512] = jnp.concatenate([eh[:, :64], oh[:, :64]], axis=1)
        r_ref[HROWS:ROWS, base + FULL : base + 512] = jnp.concatenate([eh[:, 64:], oh[:, 64:]], axis=1)

    n_col = 2 * ROWS
    row = lax.broadcasted_iota(jnp.int32, (n_col, ROWS), 0)
    r = lax.broadcasted_iota(jnp.int32, (n_col, ROWS), 1)
    h = (r >= HROWS).astype(jnp.int32)
    q = r - HROWS * h
    pick = (row == 15 * ((q * 205) >> 10) + q + HALF * h + CAP * core).astype(F32).astype(BF)

    grads = []
    for wd, sg, su, wg, wu in ((wd0, sg0, su0, wg0, wu0), (wd1, sg1, su1, wg1, wu1)):
        hidden = nt(wd[...], r_ref[...])
        g = jnp.dot(sg[...], pick, preferred_element_type=F32)
        u = jnp.dot(su[...], pick, preferred_element_type=F32)
        sig = 1.0 / (1.0 + jnp.exp(-g))
        gate = hidden * u * sig * (1.0 + g * (1.0 - sig))
        up = hidden * g * sig
        grads.append((gate.T.astype(BF), wg))
        grads.append((up.T.astype(BF), wu))

    for i in range(4):
        base, even, odd = i * PAIR, 2 * i * PIECE, (2 * i + 1) * PIECE
        acc = None
        for grad, w in grads:
            term = jnp.dot(grad, w[:, base : base + PAIR], preferred_element_type=F32)
            acc = term if acc is None else acc + term
        acc = acc.astype(BF)
        for j in range(3):
            out_ref[even + j * ROWS : even + (j + 1) * ROWS, :] = acc[:, 128 * j : 128 * (j + 1)]
            out_ref[odd + j * ROWS : odd + (j + 1) * ROWS, :] = acc[:, 512 + 128 * j : 512 + 128 * (j + 1)]
        lo = acc[0:HROWS, FULL:512]
        hi = acc[HROWS:ROWS, FULL:512]
        out_ref[even + 3 * ROWS : even + PIECE, :] = jnp.concatenate([lo[:, :64], hi[:, :64]], axis=1)
        out_ref[odd + 3 * ROWS : odd + PIECE, :] = jnp.concatenate([lo[:, 64:], hi[:, 64:]], axis=1)


def unsort_kernel(in_ref, out_ref):
    rows = GRP * HALF
    n_out = GRP * BLK
    q = lax.broadcasted_iota(jnp.int32, (n_out, rows), 1)
    row = lax.broadcasted_iota(jnp.int32, (n_out, rows), 0)
    gap = row - 35 * ((q * 205) >> 10) - q
    res = [None, None]
    for b in range(7):
        move = (gap == HALF * b).astype(F32).astype(BF)
        cols = []
        for g in range(2):
            total = None
            for t in range(TEN):
                at = t * PIECE + b * HROWS + g * rows
                part = in_ref[at : at + rows, :].astype(F32)
                total = part if total is None else total + part
            cols.append(total.astype(BF))
        term = jnp.dot(move, jnp.concatenate(cols, axis=1), preferred_element_type=F32)
        for g in range(2):
            t = term[:, g * 128 : (g + 1) * 128]
            res[g] = t if res[g] is None else res[g] + t
    for g in range(2):
        out_ref[g * n_out : (g + 1) * n_out, :] = res[g].astype(BF)


def combine_kernel(pos_ref, in_ref, tgt_ref, out_ref):
    yl = pos_ref[1]
    t0 = tgt_ref[0:1, :]
    t1 = tgt_ref[1:2, :]
    e, k = block_ids()
    low, high = slots_of(e, k)
    hit = ((low == t0) | (low == t1)).astype(F32)
    cut = lambda a, b: jnp.where((k >= a) & (k < b), hit, 0.0).astype(BF)
    hit_high = ((high == t0) | (high == t1)).astype(F32).astype(BF)
    take = jnp.concatenate([cut(0, 10), cut(10, 20), cut(20, 30), cut(30, 35), hit_high], axis=1)
    res = tn(in_ref[...], take)
    start = pl.multiple_of(64 * yl, 64)
    for j in range(3):
        out_ref[pl.ds(pl.multiple_of(start + 128 * j, 64), 128), :] = res[:, 128 * j : 128 * (j + 1)].astype(BF)
    half = res[0:64, FULL:512] + res[64:128, 512:640]
    out_ref[pl.ds(pl.multiple_of(FULL * (1 - yl), 64), 64), :] = half.astype(BF)


def call(kernel, outs, specs, flops=0, moved=0, scratch=(), limit=16):
    many = isinstance(outs, (list, tuple))
    return pl.pallas_call(
        kernel,
        out_shape=outs,
        in_specs=specs,
        out_specs=[VM] * len(outs) if many else VM,
        scratch_shapes=list(scratch),
        cost_estimate=pl.CostEstimate(flops=flops, bytes_accessed=moved, transcendentals=0),
        compiler_params=pltpu.CompilerParams(vmem_limit_bytes=limit << 20),
    )


def sds(shape, dtype=BF):
    return jax.ShapeDtypeStruct(shape, dtype)


def swap_core(a):
    return lax.ppermute(a, "core", [(0, 1), (1, 0)])


def exchange(a, axes, n):
    blocks = a.reshape(n, a.shape[0] // n, a.shape[1])
    return lax.all_to_all(blocks, axes, split_axis=0, concat_axis=0, tiled=True).reshape(a.shape)


def shards(out_grad, gate_probs, expert_ids, saved_gate, saved_up, w_gate, w_up, w_down):
    pos = jnp.stack([lax.axis_index("x"), lax.axis_index("yl"), lax.axis_index("core")]).astype(jnp.int32)
    packed, target = call(
        pack_kernel, [sds((EXP * BLK, 128)), sds((2, TOK), jnp.int32)], [SM, VM, VM, VM], 10**9, 10**6
    )(pos, out_grad.T, gate_probs.T, expert_ids.T)
    got = exchange(packed, ("z", "yh"), EXP)
    spread = call(sort_kernel, sds((TEN * PIECE, 128)), [VM], 10**9, 10**6)(got)
    pieces = exchange(spread, ("x", "yl"), TEN)
    operands = []
    for a in (w_down, w_gate, w_up, saved_gate, saved_up):
        operands += [a, swap_core(a)]
    parts = call(
        main_kernel,
        sds((TEN * PIECE, 128)),
        [SM] + [VM] * 11,
        2 * 10**9,
        10**7,
        scratch=[pltpu.VMEM((ROWS, D), BF)],
        limit=30,
    )(pos, pieces, *operands)
    arrived = exchange(parts, ("x", "yl"), TEN)
    summed = call(unsort_kernel, sds((EXP * BLK, 128)), [VM], 10**9, 10**7)(arrived)
    back = exchange(summed, ("z", "yh"), EXP)
    out_t = call(combine_kernel, sds((FEAT, TOK)), [SM, VM, VM], 10**9, 10**6)(pos, back, target)
    return out_t.T


def solution(mesh):
    grid = Mesh(mesh.devices.reshape(8, 4, 2, 4, 2), ("z", "yh", "core", "x", "yl"))
    ex, te = ("z", "yh", "core"), ("x", "yl")
    return jax.shard_map(
        shards,
        mesh=grid,
        in_specs=(P(ex, te), P(ex, None), P(ex, None)) + (P(ex + te, None),) * 5,
        out_specs=P(ex, te),
        check_vma=False,
    )
```

time: 616 us -> 140 us (0.23)
  the two profiles are of different devices: /device:TPU:1 before, /device:TPU:16 now
where the time goes in v1:
time: 140 us; the launch traced here: 139 us
  blocking collectives  82.5 us (59%)
  local copies, waits for them, and re-layouts  17.9 us (13%)
  starting transfers between devices  15 us (11%)
  waiting for transfers between devices  13.7 us (10%)
  Pallas kernels  10 us (7%)
    all_to_all x3, blocking collectives, exchange(): lax.all_to_all(blocks, axes, split_axis=0, concat_axis=0, tiled=True)  82.5 us
    unnamed x38, local copies, waits for them, and re-layouts  17.9 us
    all_to_all x1, waiting for transfers between devices, exchange(): lax.all_to_all(blocks, axes, split_axis=0, concat_axis=0, tiled=True)  12.8 us
    ppermute x5, starting transfers between devices, swap_core(): return lax.ppermute(a, 'core', [(0, 1), (1, 0)])  10.6 us
    pallas_call x1, Pallas kernels, shards(): call(main_kernel, sds((TEN * PIECE, 128)), [SM] + [VM] * 11, 2 * 10 ** 9,...  5.62 us
    all_to_all x1, starting transfers between devices, exchange(): lax.all_to_all(blocks, axes, split_axis=0, concat_axis=0, tiled=True)  4.45 us
  transfers between devices with their start and end apart: 6, of which 2 were waited for; matrix products, arithmetic and copies ran while one was open for 0% of the time, Pallas kernels for 0%

profile of v1, /device:TPU:16, one launch (start us, length us, event | category | flops | bytes accessed | tf_op | source)
XLA Modules:
  0.0 139.4 jit_solution(12907364249143446488)
XLA Ops:
  0.0 0.1 pad_add_fusion.pos_ref
  0.1 0.0 copy-start.16
  0.1 0.9 copy-done.16
  1.0 0.0 copy-start.17
  1.0 0.7 copy-done.17
  1.7 0.0 copy-start.18
  1.7 0.7 copy-done.18
  2.3 1.5 %shard_map.82 = (bf16[1280,128]{1,0:T(8,128)(2,1)S(1)}, s32[2,128]{1,0:T(2,128)S(1)}) custom-call(s32[3]{0:T(128)S(1)} %pad_add_fusion.pos_ref, bf16[448,128]{1,0:T(8,128)(2,1)S(1)} %bitcast.23, f32[2,128]{1,0:T(2,128)S(1)} %bitcast.24, s32[2,128]{1,0:T(2,128)S(1)} %bitcast.25), custom_call_target="tpu_custom_call" | custom-call | flops 1000000000 | bytes 1000000 | tf_op jit(solution)/shard_map/pallas_call | solution.py:223
  3.9 31.1 %all_to_all.20 = bf16[32,40,128]{2,1,0:T(8,128)(2,1)S(1)} all-to-all(bf16[32,40,128]{2,1,0:T(8,128)(2,1)S(1)} %bitcast.20), channel_id=1, replica_groups=mesh['z'=8,'yh'=4,'core'=2,'x'=4,'yl'=2] {'z','yh'}, dimensions={0} | all-to-all | bytes 655360 | tf_op jit(solution)/shard_map/all_to_all | solution.py:218
  35.0 0.4 shard_map.83
  35.4 0.0 copy-start
  35.4 1.4 %copy-done = bf16[8960,128]{1,0:T(8,128)(2,1)} copy-done((bf16[8960,128]{1,0:T(8,128)(2,1)}, bf16[8960,128]{1,0:T(8,128)(2,1)S(1)}, u32[]{:S(2)}) %copy-start) | copy-done | bytes 2293784
  36.8 0.0 copy-start.1
  36.8 4.5 %all-to-all-start.1 = ((bf16[8,1120,128]{2,1,0:T(8,128)(2,1)}), bf16[8,1120,128]{2,1,0:T(8,128)(2,1)S(1)}, u32[]{:S(2)}, u32[]{:S(2)}) async-start(bf16[8,1120,128]{2,1,0:T(8,128)(2,1)} %bitcast.17), calls=%async_computation.1 | async-start | bytes 4587520 | tf_op jit(solution)/shard_map/all_to_all | solution.py:218
  41.3 0.0 copy-done.1
  41.3 1.9 %collective-permute-start = (bf16[152,3584]{1,0:T(8,128)(2,1)S(1)}, bf16[152,3584]{1,0:T(8,128)(2,1)S(1)}, u32[]{:S(2)}, u32[]{:S(2)}) collective-permute-start(bf16[152,3584]{1,0:T(8,128)(2,1)S(1)} %copy-done.1), channel_id=1, source_target_pairs={{0,8},{8,0},{1,9},{9,1},{2,10},{10,2},{3,11},{11,3},{4,12},{12,4},... | collective-permute-start | bytes 3268616 | tf_op jit(solution)/shard_map/ppermute | solution.py:213
  43.2 2.4 %collective-permute-start.1 = (bf16[152,3584]{1,0:T(8,128)(2,1)}, bf16[152,3584]{1,0:T(8,128)(2,1)S(1)}, u32[]{:S(2)}, u32[]{:S(2)}) collective-permute-start(bf16[152,3584]{1,0:T(8,128)(2,1)} %wg0.1), channel_id=1, source_target_pairs={{0,8},{8,0},{1,9},{9,1},{2,10},{10,2},{3,11},{11,3},{4,12},{12,4},... | collective-permute-start | bytes 3268616 | tf_op jit(solution)/shard_map/ppermute | solution.py:213
  45.6 1.9 %collective-permute-start.2 = (bf16[152,3584]{1,0:T(8,128)(2,1)}, bf16[152,3584]{1,0:T(8,128)(2,1)S(1)}, u32[]{:S(2)}, u32[]{:S(2)}) collective-permute-start(bf16[152,3584]{1,0:T(8,128)(2,1)} %wu0.1), channel_id=1, source_target_pairs={{0,8},{8,0},{1,9},{9,1},{2,10},{10,2},{3,11},{11,3},{4,12},{12,4},... | collective-permute-start | bytes 3268616 | tf_op jit(solution)/shard_map/ppermute | solution.py:213
  47.6 2.4 %collective-permute-start.3 = (bf16[152,640]{1,0:T(8,128)(2,1)}, bf16[152,640]{1,0:T(8,128)(2,1)S(1)}, u32[]{:S(2)}, u32[]{:S(2)}) collective-permute-start(bf16[152,640]{1,0:T(8,128)(2,1)} %sg0.1), channel_id=1, source_target_pairs={{0,8},{8,0},{1,9},{9,1},{2,10},{10,2},{3,11},{11,3},{4,12},{12,4},... | collective-permute-start | bytes 583688 | tf_op jit(solution)/shard_map/ppermute | solution.py:213
  50.0 1.9 %collective-permute-start.4 = (bf16[152,640]{1,0:T(8,128)(2,1)}, bf16[152,640]{1,0:T(8,128)(2,1)S(1)}, u32[]{:S(2)}, u32[]{:S(2)}) collective-permute-start(bf16[152,640]{1,0:T(8,128)(2,1)} %su0.1), channel_id=1, source_target_pairs={{0,8},{8,0},{1,9},{9,1},{2,10},{10,2},{3,11},{11,3},{4,12},{12,4},... | collective-permute-start | bytes 583688 | tf_op jit(solution)/shard_map/ppermute | solution.py:213
  51.9 0.0 collective-permute-done.3.sg1
  51.9 0.0 copy-start.12
  51.9 0.7 copy-done.12
  52.6 0.9 collective-permute-done.4.su1
  53.5 0.0 copy-start.14
  53.5 0.7 copy-done.14
  54.2 0.0 collective-permute-done.wd1
  54.2 0.0 copy-start.4
  54.2 1.0 copy-done.4
  55.2 0.0 collective-permute-done.1.wg1
  55.2 1.0 copy-done.6
  56.2 0.0 collective-permute-done.2.wu1
  56.2 1.0 copy-done.8
  57.2 12.8 %all-to-all-done.1 = bf16[8,1120,128]{2,1,0:T(8,128)(2,1)S(1)} async-done(((bf16[8,1120,128]{2,1,0:T(8,128)(2,1)}), bf16[8,1120,128]{2,1,0:T(8,128)(2,1)S(1)}, u32[]{:S(2)}, u32[]{:S(2)}) %all-to-all-start.1) | async-done | bytes 2293792 | tf_op jit(solution)/shard_map/all_to_all | solution.py:218
  70.0 1.2 copy-done.2
  71.2 1.2 copy-done.3
  72.5 1.2 copy-done.5
  73.7 1.2 copy-done.7
  74.9 1.2 copy-done.9
  76.2 0.9 copy-done.10
  77.1 0.9 copy-done.11
  78.0 0.9 copy-done.13
  79.0 0.9 copy-done.15
  79.9 5.6 %shard_map.84 = bf16[8960,128]{1,0:T(8,128)(2,1)S(1)} custom-call(s32[3]{0:T(128)S(1)} %pad_add_fusion.pos_ref, bf16[8960,128]{1,0:T(8,128)(2,1)S(1)} %bitcast.15, bf16[152,3584]{1,0:T(8,128)(2,1)S(1)} %copy-done.1, bf16[152,3584]{1,0:T(8,128)(2,1)S(1)} %copy-done.5, bf16[152,3584]{1,0:T(8,128)(2,1)S(1)} %copy-done.2, bf16[152,3584]{1,0:T(8,128)(2,1)S(1)} %copy-done.7, ...), custom_call_target="tpu_custom_call" | custom-call | flops 2000000000 | bytes 10000000 | tf_op jit(solution)/shard_map/pallas_call | solution.py:232
  85.5 32.0 %all_to_all.21 = bf16[8,1120,128]{2,1,0:T(8,128)(2,1)S(1)} all-to-all(bf16[8,1120,128]{2,1,0:T(8,128)(2,1)S(1)} %bitcast.16), channel_id=1, replica_groups=mesh['z'=8,'yh'=4,'core'=2,'x'=4,'yl'=2] {'x','yl'}, dimensions={0} | all-to-all | bytes 4587520 | tf_op jit(solution)/shard_map/all_to_all | solution.py:218
  117.5 0.9 shard_map.85
  118.4 19.4 %all_to_all.22 = bf16[32,40,128]{2,1,0:T(8,128)(2,1)S(1)} all-to-all(bf16[32,40,128]{2,1,0:T(8,128)(2,1)S(1)} %bitcast.22), channel_id=1, replica_groups=mesh['z'=8,'yh'=4,'core'=2,'x'=4,'yl'=2] {'z','yh'}, dimensions={0} | all-to-all | bytes 655360 | tf_op jit(solution)/shard_map/all_to_all | solution.py:218
  137.8 1.7 %shard_map.86 = bf16[448,128]{1,0:T(8,128)(2,1)} custom-call(s32[3]{0:T(128)S(1)} %pad_add_fusion.pos_ref, bf16[1280,128]{1,0:T(8,128)(2,1)S(1)} %bitcast.19, s32[2,128]{1,0:T(2,128)S(1)} %get-tuple-element.8.tgt_ref), custom_call_target="tpu_custom_call" | custom-call | flops 1000000000 | bytes 1000000 | tf_op jit(solution)/shard_map/pallas_call | solution.py:244
  (11 shorter events, 0.0 us)
Async XLA Ops:
  0.1 0.9 copy-start.16
  1.0 0.7 copy-start.17
  1.7 0.7 copy-start.18
  35.4 1.4 %copy-start = (bf16[8960,128]{1,0:T(8,128)(2,1)}, bf16[8960,128]{1,0:T(8,128)(2,1)S(1)}, u32[]{:S(2)}) copy-start(bf16[8960,128]{1,0:T(8,128)(2,1)S(1)} %shard_map.83) | copy-start | bytes 6881284
  36.8 4.5 %copy-start.1 = (bf16[152,3584]{1,0:T(8,128)(2,1)S(1)}, bf16[152,3584]{1,0:T(8,128)(2,1)}, u32[]{:S(2)}) copy-start(bf16[152,3584]{1,0:T(8,128)(2,1)} %wd0.1) | copy-start | bytes 3268612
  36.8 33.1 %all-to-all-start.1 = ((bf16[8,1120,128]{2,1,0:T(8,128)(2,1)}), bf16[8,1120,128]{2,1,0:T(8,128)(2,1)S(1)}, u32[]{:S(2)}, u32[]{:S(2)}) async-start(bf16[8,1120,128]{2,1,0:T(8,128)(2,1)} %bitcast.17), calls=%async_computation.1 | async-start | bytes 4587520 | tf_op jit(solution)/shard_map/all_to_all | solution.py:218
  41.3 12.9 %collective-permute-start = (bf16[152,3584]{1,0:T(8,128)(2,1)S(1)}, bf16[152,3584]{1,0:T(8,128)(2,1)S(1)}, u32[]{:S(2)}, u32[]{:S(2)}) collective-permute-start(bf16[152,3584]{1,0:T(8,128)(2,1)S(1)} %copy-done.1), channel_id=1, source_target_pairs={{0,8},{8,0},{1,9},{9,1},{2,10},{10,2},{3,11},{11,3},{4,12},{12,4},... | collective-permute-start | bytes 3268616 | tf_op jit(solution)/shard_map/ppermute | solution.py:213
  43.2 12.0 %collective-permute-start.1 = (bf16[152,3584]{1,0:T(8,128)(2,1)}, bf16[152,3584]{1,0:T(8,128)(2,1)S(1)}, u32[]{:S(2)}, u32[]{:S(2)}) collective-permute-start(bf16[152,3584]{1,0:T(8,128)(2,1)} %wg0.1), channel_id=1, source_target_pairs={{0,8},{8,0},{1,9},{9,1},{2,10},{10,2},{3,11},{11,3},{4,12},{12,4},... | collective-permute-start | bytes 3268616 | tf_op jit(solution)/shard_map/ppermute | solution.py:213
  45.6 10.6 %collective-permute-start.2 = (bf16[152,3584]{1,0:T(8,128)(2,1)}, bf16[152,3584]{1,0:T(8,128)(2,1)S(1)}, u32[]{:S(2)}, u32[]{:S(2)}) collective-permute-start(bf16[152,3584]{1,0:T(8,128)(2,1)} %wu0.1), channel_id=1, source_target_pairs={{0,8},{8,0},{1,9},{9,1},{2,10},{10,2},{3,11},{11,3},{4,12},{12,4},... | collective-permute-start | bytes 3268616 | tf_op jit(solution)/shard_map/ppermute | solution.py:213
  47.6 4.3 %collective-permute-start.3 = (bf16[152,640]{1,0:T(8,128)(2,1)}, bf16[152,640]{1,0:T(8,128)(2,1)S(1)}, u32[]{:S(2)}, u32[]{:S(2)}) collective-permute-start(bf16[152,640]{1,0:T(8,128)(2,1)} %sg0.1), channel_id=1, source_target_pairs={{0,8},{8,0},{1,9},{9,1},{2,10},{10,2},{3,11},{11,3},{4,12},{12,4},... | collective-permute-start | bytes 583688 | tf_op jit(solution)/shard_map/ppermute | solution.py:213
  50.0 3.5 %collective-permute-start.4 = (bf16[152,640]{1,0:T(8,128)(2,1)}, bf16[152,640]{1,0:T(8,128)(2,1)S(1)}, u32[]{:S(2)}, u32[]{:S(2)}) collective-permute-start(bf16[152,640]{1,0:T(8,128)(2,1)} %su0.1), channel_id=1, source_target_pairs={{0,8},{8,0},{1,9},{9,1},{2,10},{10,2},{3,11},{11,3},{4,12},{12,4},... | collective-permute-start | bytes 583688 | tf_op jit(solution)/shard_map/ppermute | solution.py:213
  51.9 0.7 copy-start.12
  53.5 0.7 copy-start.14
  54.2 1.0 copy-start.4
  55.2 1.0 copy-start.6
  56.2 1.0 copy-start.8
  70.0 1.2 copy-start.2
  71.2 1.2 copy-start.3
  72.5 1.2 copy-start.5
  73.7 1.2 copy-start.7
  74.9 1.2 copy-start.9
  76.2 0.9 copy-start.10
  77.1 0.9 copy-start.11
  78.0 0.9 copy-start.13
  79.0 0.9 copy-start.15

commit v2 on v1

--- a/solution.py
+++ b/solution.py
@@ -10,6 +10,8 @@
 BLK = 40
 EXP = 32
 TEN = 8
+BIG = 62 * 10**6
+SMALL = 16 * 10**6
 TOK = 128
 FEAT = 448
 FULL = 384
@@ -25,6 +27,7 @@
 F32 = jnp.float32
 VM = pl.BlockSpec(memory_space=pltpu.VMEM)
 SM = pl.BlockSpec(memory_space=pltpu.SMEM)
+HB = pl.BlockSpec(memory_space=pltpu.HBM)
 
 
 def nt(a, b):
@@ -48,8 +51,17 @@
     return low, high
 
 
-def pack_kernel(pos_ref, xt_ref, gt_ref, et_ref, out_ref, tgt_ref):
+def fetch(pairs, sems):
+    copies = [pltpu.make_async_copy(src, dst, sems.at[i]) for i, (src, dst) in enumerate(pairs)]
+    for copy in copies:
+        copy.start()
+    return copies
+
+
+def pack_kernel(pos_ref, xt_hbm, gt_hbm, et_hbm, out_ref, tgt_ref, xt_ref, gt_ref, et_ref, sems):
     yl = pos_ref[1]
+    for copy in fetch(((xt_hbm, xt_ref), (gt_hbm, gt_ref), (et_hbm, et_ref)), sems):
+        copy.wait()
     e0 = et_ref[0:1, :]
     e1 = et_ref[1:2, :]
     xi = lax.broadcasted_iota(jnp.int32, (EXP, TOK), 0)
@@ -85,9 +97,8 @@
     out_ref[...] = picked.astype(BF)
 
 
-def sort_kernel(in_ref, out_ref):
-    n_out, n_in = 7 * GRP * HALF, GRP * BLK
-    rows = GRP * HALF
+def sort_kernel(in_ref, out_hbm, own_ref, sems):
+    n_in, rows = GRP * BLK, GRP * HALF
     q = lax.broadcasted_iota(jnp.int32, (rows, n_in), 0)
     col = lax.broadcasted_iota(jnp.int32, (rows, n_in), 1)
     gap = col - 35 * ((q * 205) >> 10) - q
@@ -96,15 +107,31 @@
     res = jnp.dot(moves, both, preferred_element_type=F32).astype(BF)
     for b in range(7):
         for g in range(2):
-            block = res[b * rows : (b + 1) * rows, g * 128 : (g + 1) * 128]
-            for t in range(TEN):
-                at = t * PIECE + b * HROWS + g * rows
-                out_ref[at : at + rows, :] = block
-
-
-def main_kernel(pos_ref, in_ref, wd0, wd1, wg0, wg1, wu0, wu1, sg0, sg1, su0, su1, out_ref, r_ref):
+            at = b * HROWS + g * rows
+            own_ref[at : at + rows, :] = res[b * rows : (b + 1) * rows, g * 128 : (g + 1) * 128]
+    for copy in fetch([(own_ref, out_hbm.at[pl.ds(t * PIECE, PIECE), :]) for t in range(TEN)], sems):
+        copy.wait()
+
+
+def main_kernel(pos_ref, in_hbm, *refs):
+    hbm, out_hbm = refs[0:10], refs[10]
+    in_ref, r_ref, out_ref = refs[11:14]
+    vmem, sems, out_sems = refs[14:24], refs[24], refs[25]
     core = pos_ref[2]
+    piece = lambda ref, t: ref.at[pl.ds(t * PIECE, PIECE), :]
+    copies = fetch(
+        [(piece(in_hbm, t), piece(in_ref, t)) for t in range(TEN)] + list(zip(hbm, vmem)),
+        sems,
+    )
+    n_col = 2 * ROWS
+    row = lax.broadcasted_iota(jnp.int32, (n_col, ROWS), 0)
+    r = lax.broadcasted_iota(jnp.int32, (n_col, ROWS), 1)
+    h = (r >= HROWS).astype(jnp.int32)
+    q = r - HROWS * h
+    pick = (row == 15 * ((q * 205) >> 10) + q + HALF * h + CAP * core).astype(F32).astype(BF)
     for i in range(4):
+        copies[2 * i].wait()
+        copies[2 * i + 1].wait()
         base, even, odd = i * PAIR, 2 * i * PIECE, (2 * i + 1) * PIECE
         for j in range(3):
             r_ref[:, base + 128 * j : base + 128 * (j + 1)] = in_ref[even + j * ROWS : even + (j + 1) * ROWS, :]
@@ -115,15 +142,11 @@
         r_ref[0:HROWS, base + FULL : base + 512] = jnp.concatenate([eh[:, :64], oh[:, :64]], axis=1)
         r_ref[HROWS:ROWS, base + FULL : base + 512] = jnp.concatenate([eh[:, 64:], oh[:, 64:]], axis=1)
 
-    n_col = 2 * ROWS
-    row = lax.broadcasted_iota(jnp.int32, (n_col, ROWS), 0)
-    r = lax.broadcasted_iota(jnp.int32, (n_col, ROWS), 1)
-    h = (r >= HROWS).astype(jnp.int32)
-    q = r - HROWS * h
-    pick = (row == 15 * ((q * 205) >> 10) + q + HALF * h + CAP * core).astype(F32).astype(BF)
-
     grads = []
-    for wd, sg, su, wg, wu in ((wd0, sg0, su0, wg0, wu0), (wd1, sg1, su1, wg1, wu1)):
+    for i in range(2):
+        wd, sg, su, wg, wu = vmem[5 * i : 5 * i + 5]
+        for k in range(3):
+            copies[TEN + 5 * i + k].wait()
         hidden = nt(wd[...], r_ref[...])
         g = jnp.dot(sg[...], pick, preferred_element_type=F32)
         u = jnp.dot(su[...], pick, preferred_element_type=F32)
@@ -132,7 +155,10 @@
         up = hidden * g * sig
         grads.append((gate.T.astype(BF), wg))
         grads.append((up.T.astype(BF), wu))
-
+    for k in (3, 4, 8, 9):
+        copies[TEN + k].wait()
+
+    back = []
     for i in range(4):
         base, even, odd = i * PAIR, 2 * i * PIECE, (2 * i + 1) * PIECE
         acc = None
@@ -147,6 +173,12 @@
         hi = acc[HROWS:ROWS, FULL:512]
         out_ref[even + 3 * ROWS : even + PIECE, :] = jnp.concatenate([lo[:, :64], hi[:, :64]], axis=1)
         out_ref[odd + 3 * ROWS : odd + PIECE, :] = jnp.concatenate([lo[:, 64:], hi[:, 64:]], axis=1)
+        for t in (2 * i, 2 * i + 1):
+            copy = pltpu.make_async_copy(piece(out_ref, t), piece(out_hbm, t), out_sems.at[t])
+            copy.start()
+            back.append(copy)
+    for copy in back:
+        copy.wait()
 
 
 def unsort_kernel(in_ref, out_ref):
@@ -192,16 +224,16 @@
     out_ref[pl.ds(pl.multiple_of(FULL * (1 - yl), 64), 64), :] = half.astype(BF)
 
 
-def call(kernel, outs, specs, flops=0, moved=0, scratch=(), limit=16):
+def call(kernel, outs, specs, flops=0, moved=0, scratch=(), limit=BIG, out_spec=VM):
     many = isinstance(outs, (list, tuple))
     return pl.pallas_call(
         kernel,
         out_shape=outs,
         in_specs=specs,
-        out_specs=[VM] * len(outs) if many else VM,
+        out_specs=[out_spec] * len(outs) if many else out_spec,
         scratch_shapes=list(scratch),
         cost_estimate=pl.CostEstimate(flops=flops, bytes_accessed=moved, transcendentals=0),
-        compiler_params=pltpu.CompilerParams(vmem_limit_bytes=limit << 20),
+        compiler_params=pltpu.CompilerParams(vmem_limit_bytes=limit),
     )
 
 
@@ -220,28 +252,50 @@
 
 def shards(out_grad, gate_probs, expert_ids, saved_gate, saved_up, w_gate, w_up, w_down):
     pos = jnp.stack([lax.axis_index("x"), lax.axis_index("yl"), lax.axis_index("core")]).astype(jnp.int32)
+    dma = pltpu.SemaphoreType.DMA
     packed, target = call(
-        pack_kernel, [sds((EXP * BLK, 128)), sds((2, TOK), jnp.int32)], [SM, VM, VM, VM], 10**9, 10**6
+        pack_kernel,
+        [sds((EXP * BLK, 128)), sds((2, TOK), jnp.int32)],
+        [SM, HB, HB, HB],
+        10**9,
+        10**6,
+        scratch=[
+            pltpu.VMEM((FEAT, TOK), BF),
+            pltpu.VMEM((2, TOK), F32),
+            pltpu.VMEM((2, TOK), jnp.int32),
+            dma((3,)),
+        ],
     )(pos, out_grad.T, gate_probs.T, expert_ids.T)
     got = exchange(packed, ("z", "yh"), EXP)
-    spread = call(sort_kernel, sds((TEN * PIECE, 128)), [VM], 10**9, 10**6)(got)
+    spread = call(
+        sort_kernel,
+        sds((TEN * PIECE, 128)),
+        [VM],
+        10**9,
+        10**6,
+        scratch=[pltpu.VMEM((PIECE, 128), BF), dma((TEN,))],
+        out_spec=HB,
+    )(got)
     pieces = exchange(spread, ("x", "yl"), TEN)
-    operands = []
-    for a in (w_down, w_gate, w_up, saved_gate, saved_up):
-        operands += [a, swap_core(a)]
+    own = [w_down, saved_gate, saved_up, w_gate, w_up]
+    operands = own + [swap_core(a) for a in own]
     parts = call(
         main_kernel,
         sds((TEN * PIECE, 128)),
-        [SM] + [VM] * 11,
+        [SM] + [HB] * 11,
         2 * 10**9,
         10**7,
-        scratch=[pltpu.VMEM((ROWS, D), BF)],
-        limit=30,
+        scratch=[pltpu.VMEM((TEN * PIECE, 128), BF), pltpu.VMEM((ROWS, D), BF), pltpu.VMEM((TEN * PIECE, 128), BF)]
+        + [pltpu.VMEM(a.shape, BF) for a in operands]
+        + [dma((TEN + 10,)), dma((TEN,))],
+        out_spec=HB,
     )(pos, pieces, *operands)
     arrived = exchange(parts, ("x", "yl"), TEN)
-    summed = call(unsort_kernel, sds((EXP * BLK, 128)), [VM], 10**9, 10**7)(arrived)
+    summed = call(unsort_kernel, sds((EXP * BLK, 128)), [VM], 10**9, 10**7, limit=SMALL)(arrived)
     back = exchange(summed, ("z", "yh"), EXP)
-    out_t = call(combine_kernel, sds((FEAT, TOK)), [SM, VM, VM], 10**9, 10**6)(pos, back, target)
+    out_t = call(combine_kernel, sds((FEAT, TOK)), [SM, VM, VM], 10**9, 10**6, limit=SMALL)(
+        pos, back, target
+    )
     return out_t.T
 
 

time: 140 us -> 135 us (0.964)
  the two profiles are of different devices: /device:TPU:16 before, /device:TPU:1 now
where the time goes in v2:
time: 135 us; the launch traced here: 133 us
  blocking collectives  82.9 us (61%)
  Pallas kernels  17.9 us (13%)
  starting transfers between devices  17.8 us (13%)
  waiting for transfers between devices  9.82 us (7%)
  local copies, waits for them, and re-layouts  3.54 us (3%)
    all_to_all x3, blocking collectives, exchange(): lax.all_to_all(blocks, axes, split_axis=0, concat_axis=0, tiled=True)  82.9 us
    ppermute x5, starting transfers between devices, swap_core(): return lax.ppermute(a, 'core', [(0, 1), (1, 0)])  13.7 us
    pallas_call x1, Pallas kernels, shards(): call(main_kernel, sds((TEN * PIECE, 128)), [SM] + [HB] * 11, 2 * 10 ** 9,...  9.3 us
    all_to_all x1, waiting for transfers between devices, exchange(): lax.all_to_all(blocks, axes, split_axis=0, concat_axis=0, tiled=True)  8.58 us
    all_to_all x1, starting transfers between devices, exchange(): lax.all_to_all(blocks, axes, split_axis=0, concat_axis=0, tiled=True)  4.18 us
    unnamed x16, local copies, waits for them, and re-layouts  3.54 us
    pallas_call x1, Pallas kernels, shards(): call(pack_kernel, [sds((EXP * BLK, 128)), sds((2, TOK), jnp.int32)], [SM,...  3.28 us
    pallas_call x1, Pallas kernels, shards(): call(sort_kernel, sds((TEN * PIECE, 128)), [VM], 10 ** 9, 10 ** 6, scratc...  2.83 us
  transfers between devices with their start and end apart: 6, of which 2 were waited for; matrix products, arithmetic and copies ran while one was open for 0% of the time, Pallas kernels for 0%

profile of v2, /device:TPU:1, one launch (start us, length us, event | category | flops | bytes accessed | tf_op | source)
XLA Modules:
  0.0 132.8 jit_solution(2640232242680027062)
XLA Ops:
  0.0 0.6 pad_add_fusion.pos_ref
  0.6 3.3 %shard_map.82 = (bf16[1280,128]{1,0:T(8,128)(2,1)}, s32[2,128]{1,0:T(2,128)}) custom-call(s32[3]{0:T(128)} %pad_add_fusion.pos_ref, bf16[448,128]{1,0:T(8,128)(2,1)} %bitcast.23, f32[2,128]{1,0:T(2,128)} %bitcast.24, s32[2,128]{1,0:T(2,128)} %bitcast.25), custom_call_target="tpu_custom_call" | custom-call | flops 1000000000 | bytes 1000000 | tf_op jit(solution)/shard_map/pallas_call | solution.py:256
  3.9 30.2 %all_to_all.20 = bf16[32,40,128]{2,1,0:T(8,128)(2,1)} all-to-all(bf16[32,40,128]{2,1,0:T(8,128)(2,1)} %bitcast.21), channel_id=1, replica_groups=mesh['z'=8,'yh'=4,'core'=2,'x'=4,'yl'=2] {'z','yh'}, dimensions={0} | all-to-all | bytes 655360 | tf_op jit(solution)/shard_map/all_to_all | solution.py:250
  34.1 2.8 %shard_map.83 = bf16[8960,128]{1,0:T(8,128)(2,1)} custom-call(bf16[1280,128]{1,0:T(8,128)(2,1)} %bitcast.22), custom_call_target="tpu_custom_call" | custom-call | flops 1000000000 | bytes 1000000 | tf_op jit(solution)/shard_map/pallas_call | solution.py:270
  37.0 0.0 copy-start.3
  37.0 4.2 %all-to-all-start.1 = ((bf16[8,1120,128]{2,1,0:T(8,128)(2,1)}), bf16[8,1120,128]{2,1,0:T(8,128)(2,1)S(1)}, u32[]{:S(2)}, u32[]{:S(2)}) async-start(bf16[8,1120,128]{2,1,0:T(8,128)(2,1)} %bitcast.20), calls=%async_computation.1 | async-start | bytes 4587520 | tf_op jit(solution)/shard_map/all_to_all | solution.py:250
  41.2 0.0 copy-done.3
  41.2 5.0 %collective-permute-start = (bf16[152,3584]{1,0:T(8,128)(2,1)S(1)}, bf16[152,3584]{1,0:T(8,128)(2,1)S(1)}, u32[]{:S(2)}, u32[]{:S(2)}) collective-permute-start(bf16[152,3584]{1,0:T(8,128)(2,1)S(1)} %copy-done.3), channel_id=1, source_target_pairs={{0,8},{8,0},{1,9},{9,1},{2,10},{10,2},{3,11},{11,3},{4,12},{12,4},... | collective-permute-start | bytes 3268616 | tf_op jit(solution)/shard_map/ppermute | solution.py:245
  46.2 1.9 %collective-permute-start.3 = (bf16[152,3584]{1,0:T(8,128)(2,1)}, bf16[152,3584]{1,0:T(8,128)(2,1)S(1)}, u32[]{:S(2)}, u32[]{:S(2)}) collective-permute-start(bf16[152,3584]{1,0:T(8,128)(2,1)} %refs_3_.1), channel_id=1, source_target_pairs={{0,8},{8,0},{1,9},{9,1},{2,10},{10,2},{3,11},{11,3},{4,12},{12,4},... | collective-permute-start | bytes 3268616 | tf_op jit(solution)/shard_map/ppermute | solution.py:245
  48.1 2.4 %collective-permute-start.4 = (bf16[152,3584]{1,0:T(8,128)(2,1)}, bf16[152,3584]{1,0:T(8,128)(2,1)}, u32[]{:S(2)}, u32[]{:S(2)}) collective-permute-start(bf16[152,3584]{1,0:T(8,128)(2,1)} %refs_4_.1), channel_id=1, source_target_pairs={{0,8},{8,0},{1,9},{9,1},{2,10},{10,2},{3,11},{11,3},{4,12},{12,4},... | collective-permute-start | bytes 3268616 | tf_op jit(solution)/shard_map/ppermute | solution.py:245
  50.5 1.9 %collective-permute-start.1 = (bf16[152,640]{1,0:T(8,128)(2,1)}, bf16[152,640]{1,0:T(8,128)(2,1)S(1)}, u32[]{:S(2)}, u32[]{:S(2)}) collective-permute-start(bf16[152,640]{1,0:T(8,128)(2,1)} %refs_1_.1), channel_id=1, source_target_pairs={{0,8},{8,0},{1,9},{9,1},{2,10},{10,2},{3,11},{11,3},{4,12},{12,4},... | collective-permute-start | bytes 583688 | tf_op jit(solution)/shard_map/ppermute | solution.py:245
  52.4 2.4 %collective-permute-start.2 = (bf16[152,640]{1,0:T(8,128)(2,1)}, bf16[152,640]{1,0:T(8,128)(2,1)S(1)}, u32[]{:S(2)}, u32[]{:S(2)}) collective-permute-start(bf16[152,640]{1,0:T(8,128)(2,1)} %refs_2_.1), channel_id=1, source_target_pairs={{0,8},{8,0},{1,9},{9,1},{2,10},{10,2},{3,11},{11,3},{4,12},{12,4},... | collective-permute-start | bytes 583688 | tf_op jit(solution)/shard_map/ppermute | solution.py:245
  54.9 0.0 collective-permute-done.1.refs_6_
  54.9 0.0 copy-start.6
  54.9 1.2 collective-permute-done.2.refs_7_
  56.1 0.0 copy-start.7
  56.1 0.0 collective-permute-done.refs_5_
  56.1 0.0 copy-start.4
  56.1 0.0 collective-permute-done.3.refs_8_
  56.1 0.0 copy-done.6
  56.1 0.7 copy-done.7
  56.8 0.4 copy-done.4
  57.2 0.0 copy-start.5
  57.3 1.0 copy-done.5
  58.3 0.0 collective-permute-done.4.refs_9_
  58.3 8.6 %all-to-all-done.1 = bf16[8,1120,128]{2,1,0:T(8,128)(2,1)S(1)} async-done(((bf16[8,1120,128]{2,1,0:T(8,128)(2,1)}), bf16[8,1120,128]{2,1,0:T(8,128)(2,1)S(1)}, u32[]{:S(2)}, u32[]{:S(2)}) %all-to-all-start.1) | async-done | bytes 2293792 | tf_op jit(solution)/shard_map/all_to_all | solution.py:250
  66.8 0.0 copy-start.2
  66.8 1.4 %copy-done.2 = bf16[8,1120,128]{2,1,0:T(8,128)(2,1)} copy-done((bf16[8,1120,128]{2,1,0:T(8,128)(2,1)}, bf16[8,1120,128]{2,1,0:T(8,128)(2,1)S(1)}, u32[]{:S(2)}) %copy-start.2) | copy-done | bytes 2293784
  68.2 9.3 %shard_map.84 = bf16[8960,128]{1,0:T(8,128)(2,1)} custom-call(s32[3]{0:T(128)} %pad_add_fusion.pos_ref, bf16[8960,128]{1,0:T(8,128)(2,1)} %bitcast.18, bf16[152,3584]{1,0:T(8,128)(2,1)} %refs_0_.1, bf16[152,640]{1,0:T(8,128)(2,1)} %refs_1_.1, bf16[152,640]{1,0:T(8,128)(2,1)} %refs_2_.1, bf16[152,3584]{1,0:T(8,128)(2,1)} %refs_3_.1, ...), custom_call_target="tpu_custom_call" | custom-call | flops 2000000000 | bytes 10000000 | tf_op jit(solution)/shard_map/pallas_call | solution.py:282
  77.5 32.9 %all_to_all.21 = bf16[8,1120,128]{2,1,0:T(8,128)(2,1)S(1)} all-to-all(bf16[8,1120,128]{2,1,0:T(8,128)(2,1)} %bitcast.19), channel_id=1, replica_groups=mesh['z'=8,'yh'=4,'core'=2,'x'=4,'yl'=2] {'x','yl'}, dimensions={0} | all-to-all | bytes 4587520 | tf_op jit(solution)/shard_map/all_to_all | solution.py:250
  110.5 0.0 copy-start
  110.5 0.0 copy-start.1
  110.5 0.9 shard_map.85
  111.4 19.7 %all_to_all.22 = bf16[32,40,128]{2,1,0:T(8,128)(2,1)S(1)} all-to-all(bf16[32,40,128]{2,1,0:T(8,128)(2,1)S(1)} %bitcast.17), channel_id=1, replica_groups=mesh['z'=8,'yh'=4,'core'=2,'x'=4,'yl'=2] {'z','yh'}, dimensions={0} | all-to-all | bytes 655360 | tf_op jit(solution)/shard_map/all_to_all | solution.py:250
  131.1 0.0 copy-done
  131.1 0.0 copy-done.1
  131.1 1.7 %shard_map.86 = bf16[448,128]{1,0:T(8,128)(2,1)} custom-call(s32[3]{0:T(128)S(1)} %copy-done, bf16[1280,128]{1,0:T(8,128)(2,1)S(1)} %bitcast.16, s32[2,128]{1,0:T(2,128)S(1)} %copy-done.1), custom_call_target="tpu_custom_call" | custom-call | flops 1000000000 | bytes 1000000 | tf_op jit(solution)/shard_map/pallas_call | solution.py:296
Async XLA Ops:
  37.0 4.2 %copy-start.3 = (bf16[152,3584]{1,0:T(8,128)(2,1)S(1)}, bf16[152,3584]{1,0:T(8,128)(2,1)}, u32[]{:S(2)}) copy-start(bf16[152,3584]{1,0:T(8,128)(2,1)} %refs_0_.1) | copy-start | bytes 3268612
  37.0 29.9 %all-to-all-start.1 = ((bf16[8,1120,128]{2,1,0:T(8,128)(2,1)}), bf16[8,1120,128]{2,1,0:T(8,128)(2,1)S(1)}, u32[]{:S(2)}, u32[]{:S(2)}) async-start(bf16[8,1120,128]{2,1,0:T(8,128)(2,1)} %bitcast.20), calls=%async_computation.1 | async-start | bytes 4587520 | tf_op jit(solution)/shard_map/all_to_all | solution.py:250
  41.2 15.0 %collective-permute-start = (bf16[152,3584]{1,0:T(8,128)(2,1)S(1)}, bf16[152,3584]{1,0:T(8,128)(2,1)S(1)}, u32[]{:S(2)}, u32[]{:S(2)}) collective-permute-start(bf16[152,3584]{1,0:T(8,128)(2,1)S(1)} %copy-done.3), channel_id=1, source_target_pairs={{0,8},{8,0},{1,9},{9,1},{2,10},{10,2},{3,11},{11,3},{4,12},{12,4},... | collective-permute-start | bytes 3268616 | tf_op jit(solution)/shard_map/ppermute | solution.py:245
  46.2 10.0 %collective-permute-start.3 = (bf16[152,3584]{1,0:T(8,128)(2,1)}, bf16[152,3584]{1,0:T(8,128)(2,1)S(1)}, u32[]{:S(2)}, u32[]{:S(2)}) collective-permute-start(bf16[152,3584]{1,0:T(8,128)(2,1)} %refs_3_.1), channel_id=1, source_target_pairs={{0,8},{8,0},{1,9},{9,1},{2,10},{10,2},{3,11},{11,3},{4,12},{12,4},... | collective-permute-start | bytes 3268616 | tf_op jit(solution)/shard_map/ppermute | solution.py:245
  48.1 10.2 %collective-permute-start.4 = (bf16[152,3584]{1,0:T(8,128)(2,1)}, bf16[152,3584]{1,0:T(8,128)(2,1)}, u32[]{:S(2)}, u32[]{:S(2)}) collective-permute-start(bf16[152,3584]{1,0:T(8,128)(2,1)} %refs_4_.1), channel_id=1, source_target_pairs={{0,8},{8,0},{1,9},{9,1},{2,10},{10,2},{3,11},{11,3},{4,12},{12,4},... | collective-permute-start | bytes 3268616 | tf_op jit(solution)/shard_map/ppermute | solution.py:245
  50.5 4.3 %collective-permute-start.1 = (bf16[152,640]{1,0:T(8,128)(2,1)}, bf16[152,640]{1,0:T(8,128)(2,1)S(1)}, u32[]{:S(2)}, u32[]{:S(2)}) collective-permute-start(bf16[152,640]{1,0:T(8,128)(2,1)} %refs_1_.1), channel_id=1, source_target_pairs={{0,8},{8,0},{1,9},{9,1},{2,10},{10,2},{3,11},{11,3},{4,12},{12,4},... | collective-permute-start | bytes 583688 | tf_op jit(solution)/shard_map/ppermute | solution.py:245
  52.4 3.7 %collective-permute-start.2 = (bf16[152,640]{1,0:T(8,128)(2,1)}, bf16[152,640]{1,0:T(8,128)(2,1)S(1)}, u32[]{:S(2)}, u32[]{:S(2)}) collective-permute-start(bf16[152,640]{1,0:T(8,128)(2,1)} %refs_2_.1), channel_id=1, source_target_pairs={{0,8},{8,0},{1,9},{9,1},{2,10},{10,2},{3,11},{11,3},{4,12},{12,4},... | collective-permute-start | bytes 583688 | tf_op jit(solution)/shard_map/ppermute | solution.py:245
  54.9 1.3 copy-start.6
  56.1 0.7 copy-start.7
  56.1 1.1 copy-start.4
  57.2 1.0 copy-start.5
  66.8 1.4 %copy-start.2 = (bf16[8,1120,128]{2,1,0:T(8,128)(2,1)}, bf16[8,1120,128]{2,1,0:T(8,128)(2,1)S(1)}, u32[]{:S(2)}) copy-start(bf16[8,1120,128]{2,1,0:T(8,128)(2,1)S(1)} %all-to-all-done.1) | copy-start | bytes 6881284
  110.5 20.6 %copy-start = (s32[3]{0:T(128)S(1)}, s32[3]{0:T(128)}, u32[]{:S(2)}) copy-start(s32[3]{0:T(128)} %pad_add_fusion.pos_ref) | copy-start | bytes 40
  110.5 20.6 %copy-start.1 = (s32[2,128]{1,0:T(2,128)S(1)}, s32[2,128]{1,0:T(2,128)}, u32[]{:S(2)}) copy-start(s32[2,128]{1,0:T(2,128)} %get-tuple-element.8.tgt_ref) | copy-start | bytes 3076

commit v3 on v1

--- a/solution.py
+++ b/solution.py
@@ -10,21 +10,25 @@
 BLK = 40
 EXP = 32
 TEN = 8
+BIG = 62 * 10**6
+MID = 57 * 10**6
+SMALL = 16 * 10**6
 TOK = 128
 FEAT = 448
 FULL = 384
 FF = 152
-D = 3584
 PAIR = 2 * FEAT
 ROWS = EXP * CAP
 HROWS = ROWS // 2
 PIECE = 7 * HROWS
 GRP = EXP // 2
+FPAD = 160
+D = 3584
 
 BF = jnp.bfloat16
 F32 = jnp.float32
 VM = pl.BlockSpec(memory_space=pltpu.VMEM)
-SM = pl.BlockSpec(memory_space=pltpu.SMEM)
+AN = pl.BlockSpec(memory_space=pl.ANY)
 
 
 def nt(a, b):
@@ -35,9 +39,9 @@
     return lax.dot_general(a, b, (((0,), (0,)), ((), ())), preferred_element_type=F32)
 
 
-def block_ids():
-    e = lax.broadcasted_iota(jnp.int32, (EXP, BLK, TOK), 0).reshape(EXP * BLK, TOK)
-    k = lax.broadcasted_iota(jnp.int32, (EXP, BLK, TOK), 1).reshape(EXP * BLK, TOK)
+def block_ids(rows=BLK):
+    e = lax.broadcasted_iota(jnp.int32, (EXP, rows, TOK), 0).reshape(EXP * rows, TOK)
+    k = lax.broadcasted_iota(jnp.int32, (EXP, rows, TOK), 1).reshape(EXP * rows, TOK)
     return e, k
 
 
@@ -48,8 +52,8 @@
     return low, high
 
 
-def pack_kernel(pos_ref, xt_ref, gt_ref, et_ref, out_ref, tgt_ref):
-    yl = pos_ref[1]
+def pack_kernel(xt_ref, gt_ref, et_ref, out_ref, tgt_ref):
+    yl = lax.axis_index("yl")
     e0 = et_ref[0:1, :]
     e1 = et_ref[1:2, :]
     xi = lax.broadcasted_iota(jnp.int32, (EXP, TOK), 0)
@@ -86,8 +90,7 @@
 
 
 def sort_kernel(in_ref, out_ref):
-    n_out, n_in = 7 * GRP * HALF, GRP * BLK
-    rows = GRP * HALF
+    n_in, rows = GRP * BLK, GRP * HALF
     q = lax.broadcasted_iota(jnp.int32, (rows, n_in), 0)
     col = lax.broadcasted_iota(jnp.int32, (rows, n_in), 1)
     gap = col - 35 * ((q * 205) >> 10) - q
@@ -102,8 +105,40 @@
                 out_ref[at : at + rows, :] = block
 
 
-def main_kernel(pos_ref, in_ref, wd0, wd1, wg0, wg1, wu0, wu1, sg0, sg1, su0, su1, out_ref, r_ref):
-    core = pos_ref[2]
+def stack_kernel(wd0, wd1, wg0, wg1, wu0, wu1, sg0, sg1, su0, su1, w_ref, f_ref, sg_ref, su_ref):
+    def stack(ref, first, blocks):
+        for i, block in enumerate(blocks):
+            at = first + i * FPAD
+            ref[at + FPAD - 16 : at + FPAD, :] = jnp.zeros((16, ref.shape[1]), BF)
+            ref[at : at + FF, :] = block[...]
+
+    stack(w_ref, 0, (wd0, wd1, wg0, wg1, wu0, wu1))
+
+    @pl.when(pl.program_id(0) == 0)
+    def _():
+        stack(sg_ref, 0, (sg0, sg1))
+        stack(su_ref, 0, (su0, su1))
+        core = lax.axis_index("core")
+        r = lax.broadcasted_iota(jnp.int32, (ROWS, 2 * ROWS), 0)
+        col = lax.broadcasted_iota(jnp.int32, (ROWS, 2 * ROWS), 1)
+        h = (r >= HROWS).astype(jnp.int32)
+        q = r - HROWS * h
+        pick = (col == 15 * ((q * 205) >> 10) + q + HALF * h + CAP * core).astype(F32).astype(BF)
+        g = nt(pick, sg_ref[...])
+        u = nt(pick, su_ref[...])
+        sig = 1.0 / (1.0 + jnp.exp(-g))
+        f_ref[0] = u * sig * (1.0 + g * (1.0 - sig))
+        f_ref[1] = g * sig
+
+
+def main_kernel(in_ref, f_ref, w_hbm, out_ref, r_ref, w_ref, sems):
+    down, rest = 2 * FPAD, 4 * FPAD
+    copies = [
+        pltpu.make_async_copy(w_hbm.at[pl.ds(at, n), :], w_ref.at[pl.ds(at, n), :], sems.at[i])
+        for i, (at, n) in enumerate(((0, down), (down, rest)))
+    ]
+    for copy in copies:
+        copy.start()
     for i in range(4):
         base, even, odd = i * PAIR, 2 * i * PIECE, (2 * i + 1) * PIECE
         for j in range(3):
@@ -114,32 +149,13 @@
         oh = in_ref[odd + 3 * ROWS : odd + PIECE, :]
         r_ref[0:HROWS, base + FULL : base + 512] = jnp.concatenate([eh[:, :64], oh[:, :64]], axis=1)
         r_ref[HROWS:ROWS, base + FULL : base + 512] = jnp.concatenate([eh[:, 64:], oh[:, 64:]], axis=1)
-
-    n_col = 2 * ROWS
-    row = lax.broadcasted_iota(jnp.int32, (n_col, ROWS), 0)
-    r = lax.broadcasted_iota(jnp.int32, (n_col, ROWS), 1)
-    h = (r >= HROWS).astype(jnp.int32)
-    q = r - HROWS * h
-    pick = (row == 15 * ((q * 205) >> 10) + q + HALF * h + CAP * core).astype(F32).astype(BF)
-
-    grads = []
-    for wd, sg, su, wg, wu in ((wd0, sg0, su0, wg0, wu0), (wd1, sg1, su1, wg1, wu1)):
-        hidden = nt(wd[...], r_ref[...])
-        g = jnp.dot(sg[...], pick, preferred_element_type=F32)
-        u = jnp.dot(su[...], pick, preferred_element_type=F32)
-        sig = 1.0 / (1.0 + jnp.exp(-g))
-        gate = hidden * u * sig * (1.0 + g * (1.0 - sig))
-        up = hidden * g * sig
-        grads.append((gate.T.astype(BF), wg))
-        grads.append((up.T.astype(BF), wu))
-
+    copies[0].wait()
+    hidden = nt(r_ref[...], w_ref[0:down, :])
+    grads = jnp.concatenate([hidden * f_ref[0], hidden * f_ref[1]], axis=1).astype(BF)
+    copies[1].wait()
     for i in range(4):
         base, even, odd = i * PAIR, 2 * i * PIECE, (2 * i + 1) * PIECE
-        acc = None
-        for grad, w in grads:
-            term = jnp.dot(grad, w[:, base : base + PAIR], preferred_element_type=F32)
-            acc = term if acc is None else acc + term
-        acc = acc.astype(BF)
+        acc = jnp.dot(grads, w_ref[down:, base : base + PAIR], preferred_element_type=F32).astype(BF)
         for j in range(3):
             out_ref[even + j * ROWS : even + (j + 1) * ROWS, :] = acc[:, 128 * j : 128 * (j + 1)]
             out_ref[odd + j * ROWS : odd + (j + 1) * ROWS, :] = acc[:, 512 + 128 * j : 512 + 128 * (j + 1)]
@@ -174,8 +190,8 @@
         out_ref[g * n_out : (g + 1) * n_out, :] = res[g].astype(BF)
 
 
-def combine_kernel(pos_ref, in_ref, tgt_ref, out_ref):
-    yl = pos_ref[1]
+def combine_kernel(in_ref, tgt_ref, out_ref):
+    yl = lax.axis_index("yl")
     t0 = tgt_ref[0:1, :]
     t1 = tgt_ref[1:2, :]
     e, k = block_ids()
@@ -192,16 +208,18 @@
     out_ref[pl.ds(pl.multiple_of(FULL * (1 - yl), 64), 64), :] = half.astype(BF)
 
 
-def call(kernel, outs, specs, flops=0, moved=0, scratch=(), limit=16):
-    many = isinstance(outs, (list, tuple))
+def call(kernel, outs, specs, flops, moved, scratch=(), limit=SMALL, grid=(), out_specs=VM):
+    if isinstance(outs, list) and not isinstance(out_specs, list):
+        out_specs = [out_specs] * len(outs)
     return pl.pallas_call(
         kernel,
         out_shape=outs,
+        grid=grid,
         in_specs=specs,
-        out_specs=[VM] * len(outs) if many else VM,
+        out_specs=out_specs,
         scratch_shapes=list(scratch),
         cost_estimate=pl.CostEstimate(flops=flops, bytes_accessed=moved, transcendentals=0),
-        compiler_params=pltpu.CompilerParams(vmem_limit_bytes=limit << 20),
+        compiler_params=pltpu.CompilerParams(vmem_limit_bytes=limit),
     )
 
 
@@ -219,29 +237,50 @@
 
 
 def shards(out_grad, gate_probs, expert_ids, saved_gate, saved_up, w_gate, w_up, w_down):
-    pos = jnp.stack([lax.axis_index("x"), lax.axis_index("yl"), lax.axis_index("core")]).astype(jnp.int32)
     packed, target = call(
-        pack_kernel, [sds((EXP * BLK, 128)), sds((2, TOK), jnp.int32)], [SM, VM, VM, VM], 10**9, 10**6
-    )(pos, out_grad.T, gate_probs.T, expert_ids.T)
+        pack_kernel,
+        [sds((EXP * BLK, 128)), sds((2, TOK), jnp.int32)],
+        [VM, VM, VM],
+        10**9,
+        10**6,
+        limit=BIG,
+    )(out_grad.T, gate_probs.T, expert_ids.T)
     got = exchange(packed, ("z", "yh"), EXP)
-    spread = call(sort_kernel, sds((TEN * PIECE, 128)), [VM], 10**9, 10**6)(got)
+    spread = call(sort_kernel, sds((TEN * PIECE, 128)), [VM], 10**9, 3 * 10**6)(got)
     pieces = exchange(spread, ("x", "yl"), TEN)
+
     operands = []
     for a in (w_down, w_gate, w_up, saved_gate, saved_up):
         operands += [a, swap_core(a)]
+    block = pl.BlockSpec((FF, PAIR), lambda i: (0, i))
+    saved = pl.BlockSpec((FF, 2 * ROWS), lambda i: (0, 0))
+    weights, factors = call(
+        stack_kernel,
+        [sds((6 * FPAD, D)), sds((2, ROWS, 2 * FPAD), F32)],
+        [block] * 6 + [saved] * 4,
+        5 * 10**8,
+        16 * 10**6,
+        scratch=[pltpu.VMEM((2 * FPAD, 2 * ROWS), BF)] * 2,
+        limit=BIG,
+        grid=(4,),
+        out_specs=[
+            pl.BlockSpec((6 * FPAD, PAIR), lambda i: (0, i)),
+            pl.BlockSpec((2, ROWS, 2 * FPAD), lambda i: (0, 0, 0)),
+        ],
+    )(*operands)
     parts = call(
         main_kernel,
         sds((TEN * PIECE, 128)),
-        [SM] + [VM] * 11,
-        2 * 10**9,
-        10**7,
-        scratch=[pltpu.VMEM((ROWS, D), BF)],
-        limit=30,
-    )(pos, pieces, *operands)
-    arrived = exchange(parts, ("x", "yl"), TEN)
-    summed = call(unsort_kernel, sds((EXP * BLK, 128)), [VM], 10**9, 10**7)(arrived)
+        [VM, VM, AN],
+        23 * 10**8,
+        12 * 10**6,
+        scratch=[pltpu.VMEM((ROWS, D), BF), pltpu.VMEM((6 * FPAD, D), BF), pltpu.SemaphoreType.DMA((2,))],
+        limit=MID,
+    )(pieces, factors, weights)
+    home = exchange(parts, ("x", "yl"), TEN)
+    summed = call(unsort_kernel, sds((EXP * BLK, 128)), [VM], 10**9, 3 * 10**6)(home)
     back = exchange(summed, ("z", "yh"), EXP)
-    out_t = call(combine_kernel, sds((FEAT, TOK)), [SM, VM, VM], 10**9, 10**6)(pos, back, target)
+    out_t = call(combine_kernel, sds((FEAT, TOK)), [VM, VM], 10**9, 10**6)(back, target)
     return out_t.T
 
 

time: 140 us -> 132 us (0.943)
  the two profiles are of different devices: /device:TPU:16 before, /device:TPU:1 now
where the time goes in v3:
time: 132 us; the launch traced here: 129 us
  blocking collectives  82.7 us (63%)
  Pallas kernels  22.8 us (17%)
  starting transfers between devices  17.8 us (13%)
  waiting for transfers between devices  3.49 us (3%)
  local copies, waits for them, and re-layouts  2.47 us (2%)
    all_to_all x3, blocking collectives, exchange(): lax.all_to_all(blocks, axes, split_axis=0, concat_axis=0, tiled=True)  82.7 us
    ppermute x5, starting transfers between devices, swap_core(): return lax.ppermute(a, 'core', [(0, 1), (1, 0)])  13.6 us
    pallas_call x1, Pallas kernels, shards(): call(main_kernel, sds((TEN * PIECE, 128)), [VM, VM, AN], 23 * 10 ** 8, 12...  8.86 us
    pallas_call x1, Pallas kernels, shards(): call(stack_kernel, [sds((6 * FPAD, D)), sds((2, ROWS, 2 * FPAD), F32)], [...  7.5 us
    all_to_all x1, starting transfers between devices, exchange(): lax.all_to_all(blocks, axes, split_axis=0, concat_axis=0, tiled=True)  4.17 us
  transfers between devices with their start and end apart: 6, of which 2 were waited for; matrix products, arithmetic and copies ran while one was open for 0% of the time, Pallas kernels for 6%

profile of v3, /device:TPU:1, one launch (start us, length us, event | category | flops | bytes accessed | tf_op | source)
XLA Modules:
  0.0 129.4 jit_solution(12136805354071498799)
XLA Ops:
  0.0 2.6 %shard_map.82 = (bf16[1280,128]{1,0:T(8,128)(2,1)}, s32[2,128]{1,0:T(2,128)}) custom-call(bf16[448,128]{1,0:T(8,128)(2,1)} %bitcast.19, f32[2,128]{1,0:T(2,128)} %bitcast.20, s32[2,128]{1,0:T(2,128)} %bitcast.21), custom_call_target="tpu_custom_call" | custom-call | flops 1000000000 | bytes 1000000 | tf_op jit(solution)/shard_map/pallas_call | solution.py:240
  2.6 30.1 %all_to_all.20 = bf16[32,40,128]{2,1,0:T(8,128)(2,1)S(1)} all-to-all(bf16[32,40,128]{2,1,0:T(8,128)(2,1)} %bitcast.18), channel_id=1, replica_groups=mesh['z'=8,'yh'=4,'core'=2,'x'=4,'yl'=2] {'z','yh'}, dimensions={0} | all-to-all | bytes 655360 | tf_op jit(solution)/shard_map/all_to_all | solution.py:236
  32.7 1.9 %shard_map.83 = bf16[8960,128]{1,0:T(8,128)(2,1)} custom-call(bf16[1280,128]{1,0:T(8,128)(2,1)S(1)} %bitcast.14), custom_call_target="tpu_custom_call" | custom-call | flops 1000000000 | bytes 3000000 | tf_op jit(solution)/shard_map/pallas_call | solution.py:249
  34.6 0.0 copy-start.2
  34.6 4.2 %all-to-all-start.1 = ((bf16[8,1120,128]{2,1,0:T(8,128)(2,1)}), bf16[8,1120,128]{2,1,0:T(8,128)(2,1)S(1)}, u32[]{:S(2)}, u32[]{:S(2)}) async-start(bf16[8,1120,128]{2,1,0:T(8,128)(2,1)} %bitcast.5), calls=%async_computation.1 | async-start | bytes 4587520 | tf_op jit(solution)/shard_map/all_to_all | solution.py:236
  38.8 0.0 copy-done.2
  38.8 5.0 %collective-permute-start = (bf16[152,3584]{1,0:T(8,128)(2,1)S(1)}, bf16[152,3584]{1,0:T(8,128)(2,1)S(1)}, u32[]{:S(2)}, u32[]{:S(2)}) collective-permute-start(bf16[152,3584]{1,0:T(8,128)(2,1)S(1)} %copy-done.2), channel_id=1, source_target_pairs={{0,8},{8,0},{1,9},{9,1},{2,10},{10,2},{3,11},{11,3},{4,12},{12,4},... | collective-permute-start | bytes 3268616 | tf_op jit(solution)/shard_map/ppermute | solution.py:231
  43.7 1.9 %collective-permute-start.1 = (bf16[152,3584]{1,0:T(8,128)(2,1)}, bf16[152,3584]{1,0:T(8,128)(2,1)}, u32[]{:S(2)}, u32[]{:S(2)}) collective-permute-start(bf16[152,3584]{1,0:T(8,128)(2,1)} %wg0.1), channel_id=1, source_target_pairs={{0,8},{8,0},{1,9},{9,1},{2,10},{10,2},{3,11},{11,3},{4,12},{12,4},... | collective-permute-start | bytes 3268616 | tf_op jit(solution)/shard_map/ppermute | solution.py:231
  45.7 2.4 %collective-permute-start.2 = (bf16[152,3584]{1,0:T(8,128)(2,1)}, bf16[152,3584]{1,0:T(8,128)(2,1)}, u32[]{:S(2)}, u32[]{:S(2)}) collective-permute-start(bf16[152,3584]{1,0:T(8,128)(2,1)} %wu0.1), channel_id=1, source_target_pairs={{0,8},{8,0},{1,9},{9,1},{2,10},{10,2},{3,11},{11,3},{4,12},{12,4},... | collective-permute-start | bytes 3268616 | tf_op jit(solution)/shard_map/ppermute | solution.py:231
  48.1 1.9 %collective-permute-start.3 = (bf16[152,640]{1,0:T(8,128)(2,1)}, bf16[152,640]{1,0:T(8,128)(2,1)S(1)}, u32[]{:S(2)}, u32[]{:S(2)}) collective-permute-start(bf16[152,640]{1,0:T(8,128)(2,1)} %sg0.1), channel_id=1, source_target_pairs={{0,8},{8,0},{1,9},{9,1},{2,10},{10,2},{3,11},{11,3},{4,12},{12,4},... | collective-permute-start | bytes 583688 | tf_op jit(solution)/shard_map/ppermute | solution.py:231
  50.0 2.4 %collective-permute-start.4 = (bf16[152,640]{1,0:T(8,128)(2,1)}, bf16[152,640]{1,0:T(8,128)(2,1)S(1)}, u32[]{:S(2)}, u32[]{:S(2)}) collective-permute-start(bf16[152,640]{1,0:T(8,128)(2,1)} %su0.1), channel_id=1, source_target_pairs={{0,8},{8,0},{1,9},{9,1},{2,10},{10,2},{3,11},{11,3},{4,12},{12,4},... | collective-permute-start | bytes 583688 | tf_op jit(solution)/shard_map/ppermute | solution.py:231
  52.4 0.0 collective-permute-done.3.sg1
  52.4 0.0 copy-start.4
  52.5 1.2 collective-permute-done.4.su1
  53.7 0.0 copy-start.5
  53.7 0.0 collective-permute-done.wd1
  53.7 0.0 copy-start.3
  53.7 0.0 collective-permute-done.1.wg1
  53.7 0.0 collective-permute-done.2.wu1
  53.7 0.0 copy-done.4
  53.7 0.6 copy-done.5
  54.4 0.4 copy-done.3
  54.7 7.5 %shard_map.84 = (bf16[960,3584]{1,0:T(8,128)(2,1)}, f32[2,320,320]{2,1,0:T(8,128)}) custom-call(bf16[152,3584]{1,0:T(8,128)(2,1)} %wd0.1, bf16[152,3584]{1,0:T(8,128)(2,1)} %copy-done.3, bf16[152,3584]{1,0:T(8,128)(2,1)} %wg0.1, bf16[152,3584]{1,0:T(8,128)(2,1)} %collective-permute-done.1.wg1, bf16[152,3584]{1,0:T(8,128)(2,1)} %wu0.1, ...), custom_call_target="tpu_custom_call" | custom-call | flops 500000000 | bytes 16000000 | tf_op jit(solution)/shard_map/pallas_call | solution.py:257
  62.2 2.2 %all-to-all-done.1 = bf16[8,1120,128]{2,1,0:T(8,128)(2,1)S(1)} async-done(((bf16[8,1120,128]{2,1,0:T(8,128)(2,1)}), bf16[8,1120,128]{2,1,0:T(8,128)(2,1)S(1)}, u32[]{:S(2)}, u32[]{:S(2)}) %all-to-all-start.1) | async-done | bytes 2293792 | tf_op jit(solution)/shard_map/all_to_all | solution.py:236
  64.5 0.0 copy-start.1
  64.5 1.4 %copy-done.1 = bf16[8,1120,128]{2,1,0:T(8,128)(2,1)} copy-done((bf16[8,1120,128]{2,1,0:T(8,128)(2,1)}, bf16[8,1120,128]{2,1,0:T(8,128)(2,1)S(1)}, u32[]{:S(2)}) %copy-start.1) | copy-done | bytes 2293784
  65.9 8.9 %shard_map.85 = bf16[8960,128]{1,0:T(8,128)(2,1)} custom-call(bf16[8960,128]{1,0:T(8,128)(2,1)} %bitcast.16, f32[2,320,320]{2,1,0:T(8,128)} %get-tuple-element.10.f_ref, bf16[960,3584]{1,0:T(8,128)(2,1)} %get-tuple-element.11.w_hbm), custom_call_target="tpu_custom_call" | custom-call | flops 2300000000 | bytes 12000000 | tf_op jit(solution)/shard_map/pallas_call | solution.py:271
  74.8 33.0 %all_to_all.21 = bf16[8,1120,128]{2,1,0:T(8,128)(2,1)S(1)} all-to-all(bf16[8,1120,128]{2,1,0:T(8,128)(2,1)} %bitcast.17), channel_id=1, replica_groups=mesh['z'=8,'yh'=4,'core'=2,'x'=4,'yl'=2] {'x','yl'}, dimensions={0} | all-to-all | bytes 4587520 | tf_op jit(solution)/shard_map/all_to_all | solution.py:236
  107.8 0.0 copy-start
  107.8 0.9 shard_map.86
  108.6 19.7 %all_to_all.22 = bf16[32,40,128]{2,1,0:T(8,128)(2,1)S(1)} all-to-all(bf16[32,40,128]{2,1,0:T(8,128)(2,1)S(1)} %bitcast.15), channel_id=1, replica_groups=mesh['z'=8,'yh'=4,'core'=2,'x'=4,'yl'=2] {'z','yh'}, dimensions={0} | all-to-all | bytes 655360 | tf_op jit(solution)/shard_map/all_to_all | solution.py:236
  128.3 0.0 copy-done
  128.3 1.1 shard_map.87
Async XLA Ops:
  34.6 4.2 %copy-start.2 = (bf16[152,3584]{1,0:T(8,128)(2,1)S(1)}, bf16[152,3584]{1,0:T(8,128)(2,1)}, u32[]{:S(2)}) copy-start(bf16[152,3584]{1,0:T(8,128)(2,1)} %wd0.1) | copy-start | bytes 3268612
  34.6 29.9 %all-to-all-start.1 = ((bf16[8,1120,128]{2,1,0:T(8,128)(2,1)}), bf16[8,1120,128]{2,1,0:T(8,128)(2,1)S(1)}, u32[]{:S(2)}, u32[]{:S(2)}) async-start(bf16[8,1120,128]{2,1,0:T(8,128)(2,1)} %bitcast.5), calls=%async_computation.1 | async-start | bytes 4587520 | tf_op jit(solution)/shard_map/all_to_all | solution.py:236
  38.8 14.9 %collective-permute-start = (bf16[152,3584]{1,0:T(8,128)(2,1)S(1)}, bf16[152,3584]{1,0:T(8,128)(2,1)S(1)}, u32[]{:S(2)}, u32[]{:S(2)}) collective-permute-start(bf16[152,3584]{1,0:T(8,128)(2,1)S(1)} %copy-done.2), channel_id=1, source_target_pairs={{0,8},{8,0},{1,9},{9,1},{2,10},{10,2},{3,11},{11,3},{4,12},{12,4},... | collective-permute-start | bytes 3268616 | tf_op jit(solution)/shard_map/ppermute | solution.py:231
  43.7 10.0 %collective-permute-start.1 = (bf16[152,3584]{1,0:T(8,128)(2,1)}, bf16[152,3584]{1,0:T(8,128)(2,1)}, u32[]{:S(2)}, u32[]{:S(2)}) collective-permute-start(bf16[152,3584]{1,0:T(8,128)(2,1)} %wg0.1), channel_id=1, source_target_pairs={{0,8},{8,0},{1,9},{9,1},{2,10},{10,2},{3,11},{11,3},{4,12},{12,4},... | collective-permute-start | bytes 3268616 | tf_op jit(solution)/shard_map/ppermute | solution.py:231
  45.7 8.0 %collective-permute-start.2 = (bf16[152,3584]{1,0:T(8,128)(2,1)}, bf16[152,3584]{1,0:T(8,128)(2,1)}, u32[]{:S(2)}, u32[]{:S(2)}) collective-permute-start(bf16[152,3584]{1,0:T(8,128)(2,1)} %wu0.1), channel_id=1, source_target_pairs={{0,8},{8,0},{1,9},{9,1},{2,10},{10,2},{3,11},{11,3},{4,12},{12,4},... | collective-permute-start | bytes 3268616 | tf_op jit(solution)/shard_map/ppermute | solution.py:231
  48.1 4.3 %collective-permute-start.3 = (bf16[152,640]{1,0:T(8,128)(2,1)}, bf16[152,640]{1,0:T(8,128)(2,1)S(1)}, u32[]{:S(2)}, u32[]{:S(2)}) collective-permute-start(bf16[152,640]{1,0:T(8,128)(2,1)} %sg0.1), channel_id=1, source_target_pairs={{0,8},{8,0},{1,9},{9,1},{2,10},{10,2},{3,11},{11,3},{4,12},{12,4},... | collective-permute-start | bytes 583688 | tf_op jit(solution)/shard_map/ppermute | solution.py:231
  50.0 3.7 %collective-permute-start.4 = (bf16[152,640]{1,0:T(8,128)(2,1)}, bf16[152,640]{1,0:T(8,128)(2,1)S(1)}, u32[]{:S(2)}, u32[]{:S(2)}) collective-permute-start(bf16[152,640]{1,0:T(8,128)(2,1)} %su0.1), channel_id=1, source_target_pairs={{0,8},{8,0},{1,9},{9,1},{2,10},{10,2},{3,11},{11,3},{4,12},{12,4},... | collective-permute-start | bytes 583688 | tf_op jit(solution)/shard_map/ppermute | solution.py:231
  52.4 1.3 copy-start.4
  53.7 0.7 copy-start.5
  53.7 1.0 copy-start.3
  64.5 1.4 %copy-start.1 = (bf16[8,1120,128]{2,1,0:T(8,128)(2,1)}, bf16[8,1120,128]{2,1,0:T(8,128)(2,1)S(1)}, u32[]{:S(2)}) copy-start(bf16[8,1120,128]{2,1,0:T(8,128)(2,1)S(1)} %all-to-all-done.1) | copy-start | bytes 6881284
  107.8 20.5 %copy-start = (s32[2,128]{1,0:T(2,128)S(1)}, s32[2,128]{1,0:T(2,128)}, u32[]{:S(2)}) copy-start(s32[2,128]{1,0:T(2,128)} %get-tuple-element.12.tgt_ref) | copy-start | bytes 3076

commit v4 on v3

--- a/solution.py
+++ b/solution.py
@@ -11,7 +11,7 @@
 EXP = 32
 TEN = 8
 BIG = 62 * 10**6
-MID = 57 * 10**6
+MID = 50 * 10**6
 SMALL = 16 * 10**6
 TOK = 128
 FEAT = 448
@@ -140,7 +140,7 @@
     for copy in copies:
         copy.start()
     for i in range(4):
-        base, even, odd = i * PAIR, 2 * i * PIECE, (2 * i + 1) * PIECE
+        base, even, odd = i * PAIR, i * PIECE, (4 + i) * PIECE
         for j in range(3):
             r_ref[:, base + 128 * j : base + 128 * (j + 1)] = in_ref[even + j * ROWS : even + (j + 1) * ROWS, :]
             at = base + 512 + 128 * j
@@ -154,7 +154,7 @@
     grads = jnp.concatenate([hidden * f_ref[0], hidden * f_ref[1]], axis=1).astype(BF)
     copies[1].wait()
     for i in range(4):
-        base, even, odd = i * PAIR, 2 * i * PIECE, (2 * i + 1) * PIECE
+        base, even, odd = i * PAIR, i * PIECE, (4 + i) * PIECE
         acc = jnp.dot(grads, w_ref[down:, base : base + PAIR], preferred_element_type=F32).astype(BF)
         for j in range(3):
             out_ref[even + j * ROWS : even + (j + 1) * ROWS, :] = acc[:, 128 * j : 128 * (j + 1)]
@@ -247,7 +247,7 @@
     )(out_grad.T, gate_probs.T, expert_ids.T)
     got = exchange(packed, ("z", "yh"), EXP)
     spread = call(sort_kernel, sds((TEN * PIECE, 128)), [VM], 10**9, 3 * 10**6)(got)
-    pieces = exchange(spread, ("x", "yl"), TEN)
+    pieces = exchange(spread, ("yl", "x"), TEN)
 
     operands = []
     for a in (w_down, w_gate, w_up, saved_gate, saved_up):
@@ -277,7 +277,7 @@
         scratch=[pltpu.VMEM((ROWS, D), BF), pltpu.VMEM((6 * FPAD, D), BF), pltpu.SemaphoreType.DMA((2,))],
         limit=MID,
     )(pieces, factors, weights)
-    home = exchange(parts, ("x", "yl"), TEN)
+    home = exchange(parts, ("yl", "x"), TEN)
     summed = call(unsort_kernel, sds((EXP * BLK, 128)), [VM], 10**9, 3 * 10**6)(home)
     back = exchange(summed, ("z", "yh"), EXP)
     out_t = call(combine_kernel, sds((FEAT, TOK)), [VM, VM], 10**9, 10**6)(back, target)

time: 132 us -> 129 us (0.977)
  Pallas kernels: 22.8 us -> 17.8 us
  waiting for transfers between devices: 3.49 us -> 5.88 us
  blocking collectives: 82.7 us -> 80.7 us
    pallas_call x1, Pallas kernels: 8.86 us -> 5.27 us  [shards(): call(main_kernel, sds((TEN * PIECE, 128)), [VM, VM, AN], 23 * 10 ** 8, 12...]
    all_to_all x1, waiting for transfers between devices: 2.25 us -> 4.63 us  [exchange(): lax.all_to_all(blocks, axes, split_axis=0, concat_axis=0, tiled=True)]
    all_to_all x3, blocking collectives: 82.7 us -> 80.7 us  [exchange(): lax.all_to_all(blocks, axes, split_axis=0, concat_axis=0, tiled=True)]
    pallas_call x1, Pallas kernels: 1.86 us -> 0.4 us  [shards(): call(sort_kernel, sds((TEN * PIECE, 128)), [VM], 10 ** 9, 3 * 10 ** 6)(got)]
    unnamed x12 -> x14, local copies, waits for them, and re-layouts: 2.47 us -> 3.65 us
where the time goes in v4:
time: 129 us; the launch traced here: 126 us
  blocking collectives  80.7 us (63%)
  Pallas kernels  17.8 us (14%)
  starting transfers between devices  17.8 us (14%)
  waiting for transfers between devices  5.88 us (5%)
  local copies, waits for them, and re-layouts  3.65 us (3%)
    all_to_all x3, blocking collectives, exchange(): lax.all_to_all(blocks, axes, split_axis=0, concat_axis=0, tiled=True)  80.7 us
    ppermute x5, starting transfers between devices, swap_core(): return lax.ppermute(a, 'core', [(0, 1), (1, 0)])  13.6 us
    pallas_call x1, Pallas kernels, shards(): call(stack_kernel, [sds((6 * FPAD, D)), sds((2, ROWS, 2 * FPAD), F32)], [...  7.58 us
    pallas_call x1, Pallas kernels, shards(): call(main_kernel, sds((TEN * PIECE, 128)), [VM, VM, AN], 23 * 10 ** 8, 12...  5.27 us
    all_to_all x1, waiting for transfers between devices, exchange(): lax.all_to_all(blocks, axes, split_axis=0, concat_axis=0, tiled=True)  4.63 us
    all_to_all x1, starting transfers between devices, exchange(): lax.all_to_all(blocks, axes, split_axis=0, concat_axis=0, tiled=True)  4.17 us
    unnamed x14, local copies, waits for them, and re-layouts  3.65 us
    pallas_call x1, Pallas kernels, shards(): call(pack_kernel, [sds((EXP * BLK, 128)), sds((2, TOK), jnp.int32)], [VM,...  2.62 us
  transfers between devices with their start and end apart: 6, of which 2 were waited for; matrix products, arithmetic and copies ran while one was open for 0% of the time, Pallas kernels for 6%

profile of v4, /device:TPU:1, one launch (start us, length us, event | category | flops | bytes accessed | tf_op | source)
XLA Modules:
  0.0 126.0 jit_solution(15721965679240581144)
XLA Ops:
  0.0 2.6 %shard_map.82 = (bf16[1280,128]{1,0:T(8,128)(2,1)}, s32[2,128]{1,0:T(2,128)}) custom-call(bf16[448,128]{1,0:T(8,128)(2,1)} %bitcast.20, f32[2,128]{1,0:T(2,128)} %bitcast.21, s32[2,128]{1,0:T(2,128)} %bitcast.22), custom_call_target="tpu_custom_call" | custom-call | flops 1000000000 | bytes 1000000 | tf_op jit(solution)/shard_map/pallas_call | solution.py:240
  2.6 30.1 %all_to_all.20 = bf16[32,40,128]{2,1,0:T(8,128)(2,1)S(1)} all-to-all(bf16[32,40,128]{2,1,0:T(8,128)(2,1)} %bitcast.19), channel_id=1, replica_groups=mesh['z'=8,'yh'=4,'core'=2,'x'=4,'yl'=2] {'z','yh'}, dimensions={0} | all-to-all | bytes 655360 | tf_op jit(solution)/shard_map/all_to_all | solution.py:236
  32.7 0.4 shard_map.83
  33.1 0.0 copy-start
  33.1 1.4 %copy-done = bf16[8960,128]{1,0:T(8,128)(2,1)} copy-done((bf16[8960,128]{1,0:T(8,128)(2,1)}, bf16[8960,128]{1,0:T(8,128)(2,1)S(1)}, u32[]{:S(2)}) %copy-start) | copy-done | bytes 2293784
  34.6 0.0 copy-start.3
  34.6 4.2 %all-to-all-start.1 = ((bf16[8,1120,128]{2,1,0:T(8,128)(2,1)}), bf16[8,1120,128]{2,1,0:T(8,128)(2,1)S(1)}, u32[]{:S(2)}, u32[]{:S(2)}) async-start(bf16[8,1120,128]{2,1,0:T(8,128)(2,1)} %bitcast.14), calls=%async_computation.1 | async-start | bytes 4587520 | tf_op jit(solution)/shard_map/all_to_all | solution.py:236
  38.8 0.0 copy-done.3
  38.8 5.0 %collective-permute-start = (bf16[152,3584]{1,0:T(8,128)(2,1)S(1)}, bf16[152,3584]{1,0:T(8,128)(2,1)S(1)}, u32[]{:S(2)}, u32[]{:S(2)}) collective-permute-start(bf16[152,3584]{1,0:T(8,128)(2,1)S(1)} %copy-done.3), channel_id=1, source_target_pairs={{0,8},{8,0},{1,9},{9,1},{2,10},{10,2},{3,11},{11,3},{4,12},{12,4},... | collective-permute-start | bytes 3268616 | tf_op jit(solution)/shard_map/ppermute | solution.py:231
  43.7 1.9 %collective-permute-start.1 = (bf16[152,3584]{1,0:T(8,128)(2,1)}, bf16[152,3584]{1,0:T(8,128)(2,1)}, u32[]{:S(2)}, u32[]{:S(2)}) collective-permute-start(bf16[152,3584]{1,0:T(8,128)(2,1)} %wg0.1), channel_id=1, source_target_pairs={{0,8},{8,0},{1,9},{9,1},{2,10},{10,2},{3,11},{11,3},{4,12},{12,4},... | collective-permute-start | bytes 3268616 | tf_op jit(solution)/shard_map/ppermute | solution.py:231
  45.7 2.4 %collective-permute-start.2 = (bf16[152,3584]{1,0:T(8,128)(2,1)}, bf16[152,3584]{1,0:T(8,128)(2,1)}, u32[]{:S(2)}, u32[]{:S(2)}) collective-permute-start(bf16[152,3584]{1,0:T(8,128)(2,1)} %wu0.1), channel_id=1, source_target_pairs={{0,8},{8,0},{1,9},{9,1},{2,10},{10,2},{3,11},{11,3},{4,12},{12,4},... | collective-permute-start | bytes 3268616 | tf_op jit(solution)/shard_map/ppermute | solution.py:231
  48.1 1.9 %collective-permute-start.3 = (bf16[152,640]{1,0:T(8,128)(2,1)}, bf16[152,640]{1,0:T(8,128)(2,1)S(1)}, u32[]{:S(2)}, u32[]{:S(2)}) collective-permute-start(bf16[152,640]{1,0:T(8,128)(2,1)} %sg0.1), channel_id=1, source_target_pairs={{0,8},{8,0},{1,9},{9,1},{2,10},{10,2},{3,11},{11,3},{4,12},{12,4},... | collective-permute-start | bytes 583688 | tf_op jit(solution)/shard_map/ppermute | solution.py:231
  50.0 2.4 %collective-permute-start.4 = (bf16[152,640]{1,0:T(8,128)(2,1)}, bf16[152,640]{1,0:T(8,128)(2,1)S(1)}, u32[]{:S(2)}, u32[]{:S(2)}) collective-permute-start(bf16[152,640]{1,0:T(8,128)(2,1)} %su0.1), channel_id=1, source_target_pairs={{0,8},{8,0},{1,9},{9,1},{2,10},{10,2},{3,11},{11,3},{4,12},{12,4},... | collective-permute-start | bytes 583688 | tf_op jit(solution)/shard_map/ppermute | solution.py:231
  52.4 0.0 collective-permute-done.3.sg1
  52.4 0.0 copy-start.5
  52.4 1.2 collective-permute-done.4.su1
  53.7 0.0 copy-start.6
  53.7 0.0 collective-permute-done.wd1
  53.7 0.0 copy-start.4
  53.7 0.0 collective-permute-done.1.wg1
  53.7 0.0 collective-permute-done.2.wu1
  53.7 0.0 copy-done.5
  53.7 0.6 copy-done.6
  54.4 0.4 copy-done.4
  54.7 7.6 %shard_map.84 = (bf16[960,3584]{1,0:T(8,128)(2,1)}, f32[2,320,320]{2,1,0:T(8,128)}) custom-call(bf16[152,3584]{1,0:T(8,128)(2,1)} %wd0.1, bf16[152,3584]{1,0:T(8,128)(2,1)} %copy-done.4, bf16[152,3584]{1,0:T(8,128)(2,1)} %wg0.1, bf16[152,3584]{1,0:T(8,128)(2,1)} %collective-permute-done.1.wg1, bf16[152,3584]{1,0:T(8,128)(2,1)} %wu0.1, ...), custom_call_target="tpu_custom_call" | custom-call | flops 500000000 | bytes 16000000 | tf_op jit(solution)/shard_map/pallas_call | solution.py:257
  62.3 4.6 %all-to-all-done.1 = bf16[8,1120,128]{2,1,0:T(8,128)(2,1)S(1)} async-done(((bf16[8,1120,128]{2,1,0:T(8,128)(2,1)}), bf16[8,1120,128]{2,1,0:T(8,128)(2,1)S(1)}, u32[]{:S(2)}, u32[]{:S(2)}) %all-to-all-start.1) | async-done | bytes 2293792 | tf_op jit(solution)/shard_map/all_to_all | solution.py:236
  66.9 0.0 copy-start.1
  66.9 1.2 copy-done.1
  68.1 5.3 %shard_map.85 = bf16[8960,128]{1,0:T(8,128)(2,1)S(1)} custom-call(bf16[8960,128]{1,0:T(8,128)(2,1)S(1)} %bitcast.12, f32[2,320,320]{2,1,0:T(8,128)S(1)} %copy-done.1, bf16[960,3584]{1,0:T(8,128)(2,1)} %get-tuple-element.11.w_hbm), custom_call_target="tpu_custom_call" | custom-call | flops 2300000000 | bytes 12000000 | tf_op jit(solution)/shard_map/pallas_call | solution.py:271
  73.4 31.7 %all_to_all.21 = bf16[8,1120,128]{2,1,0:T(8,128)(2,1)S(1)} all-to-all(bf16[8,1120,128]{2,1,0:T(8,128)(2,1)S(1)} %bitcast.13), channel_id=1, replica_groups=mesh['z'=8,'yh'=4,'core'=2,'x'=4,'yl'=2] {'yl','x'}, dimensions={0} | all-to-all | bytes 4587520 | tf_op jit(solution)/shard_map/all_to_all | solution.py:236
  105.2 0.0 copy-start.2
  105.2 0.9 shard_map.86
  106.0 18.8 %all_to_all.22 = bf16[32,40,128]{2,1,0:T(8,128)(2,1)S(1)} all-to-all(bf16[32,40,128]{2,1,0:T(8,128)(2,1)S(1)} %bitcast.18), channel_id=1, replica_groups=mesh['z'=8,'yh'=4,'core'=2,'x'=4,'yl'=2] {'z','yh'}, dimensions={0} | all-to-all | bytes 655360 | tf_op jit(solution)/shard_map/all_to_all | solution.py:236
  124.8 0.0 copy-done.2
  124.8 1.1 shard_map.87
Async XLA Ops:
  33.1 1.4 %copy-start = (bf16[8960,128]{1,0:T(8,128)(2,1)}, bf16[8960,128]{1,0:T(8,128)(2,1)S(1)}, u32[]{:S(2)}) copy-start(bf16[8960,128]{1,0:T(8,128)(2,1)S(1)} %shard_map.83) | copy-start | bytes 6881284
  34.6 4.2 %copy-start.3 = (bf16[152,3584]{1,0:T(8,128)(2,1)S(1)}, bf16[152,3584]{1,0:T(8,128)(2,1)}, u32[]{:S(2)}) copy-start(bf16[152,3584]{1,0:T(8,128)(2,1)} %wd0.1) | copy-start | bytes 3268612
  34.6 32.4 %all-to-all-start.1 = ((bf16[8,1120,128]{2,1,0:T(8,128)(2,1)}), bf16[8,1120,128]{2,1,0:T(8,128)(2,1)S(1)}, u32[]{:S(2)}, u32[]{:S(2)}) async-start(bf16[8,1120,128]{2,1,0:T(8,128)(2,1)} %bitcast.14), calls=%async_computation.1 | async-start | bytes 4587520 | tf_op jit(solution)/shard_map/all_to_all | solution.py:236
  38.8 14.9 %collective-permute-start = (bf16[152,3584]{1,0:T(8,128)(2,1)S(1)}, bf16[152,3584]{1,0:T(8,128)(2,1)S(1)}, u32[]{:S(2)}, u32[]{:S(2)}) collective-permute-start(bf16[152,3584]{1,0:T(8,128)(2,1)S(1)} %copy-done.3), channel_id=1, source_target_pairs={{0,8},{8,0},{1,9},{9,1},{2,10},{10,2},{3,11},{11,3},{4,12},{12,4},... | collective-permute-start | bytes 3268616 | tf_op jit(solution)/shard_map/ppermute | solution.py:231
  43.7 10.0 %collective-permute-start.1 = (bf16[152,3584]{1,0:T(8,128)(2,1)}, bf16[152,3584]{1,0:T(8,128)(2,1)}, u32[]{:S(2)}, u32[]{:S(2)}) collective-permute-start(bf16[152,3584]{1,0:T(8,128)(2,1)} %wg0.1), channel_id=1, source_target_pairs={{0,8},{8,0},{1,9},{9,1},{2,10},{10,2},{3,11},{11,3},{4,12},{12,4},... | collective-permute-start | bytes 3268616 | tf_op jit(solution)/shard_map/ppermute | solution.py:231
  45.7 8.0 %collective-permute-start.2 = (bf16[152,3584]{1,0:T(8,128)(2,1)}, bf16[152,3584]{1,0:T(8,128)(2,1)}, u32[]{:S(2)}, u32[]{:S(2)}) collective-permute-start(bf16[152,3584]{1,0:T(8,128)(2,1)} %wu0.1), channel_id=1, source_target_pairs={{0,8},{8,0},{1,9},{9,1},{2,10},{10,2},{3,11},{11,3},{4,12},{12,4},... | collective-permute-start | bytes 3268616 | tf_op jit(solution)/shard_map/ppermute | solution.py:231
  48.1 4.3 %collective-permute-start.3 = (bf16[152,640]{1,0:T(8,128)(2,1)}, bf16[152,640]{1,0:T(8,128)(2,1)S(1)}, u32[]{:S(2)}, u32[]{:S(2)}) collective-permute-start(bf16[152,640]{1,0:T(8,128)(2,1)} %sg0.1), channel_id=1, source_target_pairs={{0,8},{8,0},{1,9},{9,1},{2,10},{10,2},{3,11},{11,3},{4,12},{12,4},... | collective-permute-start | bytes 583688 | tf_op jit(solution)/shard_map/ppermute | solution.py:231
  50.0 3.7 %collective-permute-start.4 = (bf16[152,640]{1,0:T(8,128)(2,1)}, bf16[152,640]{1,0:T(8,128)(2,1)S(1)}, u32[]{:S(2)}, u32[]{:S(2)}) collective-permute-start(bf16[152,640]{1,0:T(8,128)(2,1)} %su0.1), channel_id=1, source_target_pairs={{0,8},{8,0},{1,9},{9,1},{2,10},{10,2},{3,11},{11,3},{4,12},{12,4},... | collective-permute-start | bytes 583688 | tf_op jit(solution)/shard_map/ppermute | solution.py:231
  52.4 1.3 %copy-start.5 = (bf16[152,640]{1,0:T(8,128)(2,1)}, bf16[152,640]{1,0:T(8,128)(2,1)S(1)}, u32[]{:S(2)}) copy-start(bf16[152,640]{1,0:T(8,128)(2,1)S(1)} %collective-permute-done.3.sg1) | copy-start | bytes 583684
  53.7 0.7 copy-start.6
  53.7 1.0 copy-start.4
  66.9 1.2 copy-start.1
  105.2 19.7 %copy-start.2 = (s32[2,128]{1,0:T(2,128)S(1)}, s32[2,128]{1,0:T(2,128)}, u32[]{:S(2)}) copy-start(s32[2,128]{1,0:T(2,128)} %get-tuple-element.12.tgt_ref) | copy-start | bytes 3076

commit v5 on v4

--- a/solution.py
+++ b/solution.py
@@ -40,7 +40,8 @@
 
 
 def block_ids(rows=BLK):
-    e = lax.broadcasted_iota(jnp.int32, (EXP, rows, TOK), 0).reshape(EXP * rows, TOK)
+    p = lax.broadcasted_iota(jnp.int32, (EXP, rows, TOK), 0).reshape(EXP * rows, TOK)
+    e = 4 * (p & 7) + (p >> 3)
     k = lax.broadcasted_iota(jnp.int32, (EXP, rows, TOK), 1).reshape(EXP * rows, TOK)
     return e, k
 
@@ -105,7 +106,8 @@
                 out_ref[at : at + rows, :] = block
 
 
-def stack_kernel(wd0, wd1, wg0, wg1, wu0, wu1, sg0, sg1, su0, su1, w_ref, f_ref, sg_ref, su_ref):
+def stack_kernel(wd0, wd1, wg0, wg1, wu0, wu1, sg0, sg1, su0, su1, w_ref, sg_ref, su_ref, f_ref):
+    step = pl.program_id(0)
     def stack(ref, first, blocks):
         for i, block in enumerate(blocks):
             at = first + i * FPAD
@@ -114,7 +116,7 @@
 
     stack(w_ref, 0, (wd0, wd1, wg0, wg1, wu0, wu1))
 
-    @pl.when(pl.program_id(0) == 0)
+    @pl.when(step == 0)
     def _():
         stack(sg_ref, 0, (sg0, sg1))
         stack(su_ref, 0, (su0, su1))
@@ -123,20 +125,29 @@
         col = lax.broadcasted_iota(jnp.int32, (ROWS, 2 * ROWS), 1)
         h = (r >= HROWS).astype(jnp.int32)
         q = r - HROWS * h
-        pick = (col == 15 * ((q * 205) >> 10) + q + HALF * h + CAP * core).astype(F32).astype(BF)
+        p = (q * 205) >> 10
+        source = 4 * (p & 7) + (p >> 3)
+        pick = (col == 2 * CAP * source + (q - HALF * p) + HALF * h + CAP * core).astype(F32).astype(BF)
         g = nt(pick, sg_ref[...])
         u = nt(pick, su_ref[...])
         sig = 1.0 / (1.0 + jnp.exp(-g))
-        f_ref[0] = u * sig * (1.0 + g * (1.0 - sig))
-        f_ref[1] = g * sig
-
-
-def main_kernel(in_ref, f_ref, w_hbm, out_ref, r_ref, w_ref, sems):
+        for i, factor in enumerate((u * sig * (1.0 + g * (1.0 - sig)), g * sig)):
+            high = factor.astype(BF)
+            f_ref[2 * i] = high
+            f_ref[2 * i + 1] = (factor - high.astype(F32)).astype(BF)
+
+    w_ref[6 * FPAD :, 0:FULL] = jnp.concatenate([f_ref[step], jnp.zeros((ROWS, FULL - 2 * FPAD), BF)], axis=1)
+
+
+def main_kernel(in_ref, w_hbm, out_ref, r_ref, w_ref, f_ref, sems):
     down, rest = 2 * FPAD, 4 * FPAD
-    copies = [
-        pltpu.make_async_copy(w_hbm.at[pl.ds(at, n), :], w_ref.at[pl.ds(at, n), :], sems.at[i])
-        for i, (at, n) in enumerate(((0, down), (down, rest)))
-    ]
+    pairs = [(w_hbm.at[pl.ds(0, down), :], w_ref.at[pl.ds(0, down), :])]
+    for i in range(4):
+        pairs.append((w_hbm.at[pl.ds(down + rest, ROWS), pl.ds(i * PAIR, FULL)], f_ref.at[i]))
+    for i in range(4):
+        at = (pl.ds(down, rest), pl.ds(i * PAIR, PAIR))
+        pairs.append((w_hbm.at[at], w_ref.at[at]))
+    copies = [pltpu.make_async_copy(src, dst, sems.at[i]) for i, (src, dst) in enumerate(pairs)]
     for copy in copies:
         copy.start()
     for i in range(4):
@@ -151,10 +162,13 @@
         r_ref[HROWS:ROWS, base + FULL : base + 512] = jnp.concatenate([eh[:, 64:], oh[:, 64:]], axis=1)
     copies[0].wait()
     hidden = nt(r_ref[...], w_ref[0:down, :])
-    grads = jnp.concatenate([hidden * f_ref[0], hidden * f_ref[1]], axis=1).astype(BF)
-    copies[1].wait()
+    for copy in copies[1:5]:
+        copy.wait()
+    part = lambda i: f_ref[i, :, 0:down].astype(F32)
+    grads = jnp.concatenate([hidden * (part(0) + part(1)), hidden * (part(2) + part(3))], axis=1).astype(BF)
     for i in range(4):
-        base, even, odd = i * PAIR, i * PIECE, (4 + i) * PIECE
+        base, even, odd = i * PAIR, 2 * i * PIECE, (2 * i + 1) * PIECE
+        copies[5 + i].wait()
         acc = jnp.dot(grads, w_ref[down:, base : base + PAIR], preferred_element_type=F32).astype(BF)
         for j in range(3):
             out_ref[even + j * ROWS : even + (j + 1) * ROWS, :] = acc[:, 128 * j : 128 * (j + 1)]
@@ -245,7 +259,7 @@
         10**6,
         limit=BIG,
     )(out_grad.T, gate_probs.T, expert_ids.T)
-    got = exchange(packed, ("z", "yh"), EXP)
+    got = exchange(packed, ("yh", "z"), EXP)
     spread = call(sort_kernel, sds((TEN * PIECE, 128)), [VM], 10**9, 3 * 10**6)(got)
     pieces = exchange(spread, ("yl", "x"), TEN)
 
@@ -254,32 +268,34 @@
         operands += [a, swap_core(a)]
     block = pl.BlockSpec((FF, PAIR), lambda i: (0, i))
     saved = pl.BlockSpec((FF, 2 * ROWS), lambda i: (0, 0))
-    weights, factors = call(
+    weights = call(
         stack_kernel,
-        [sds((6 * FPAD, D)), sds((2, ROWS, 2 * FPAD), F32)],
+        sds((6 * FPAD + ROWS, D)),
         [block] * 6 + [saved] * 4,
         5 * 10**8,
         16 * 10**6,
-        scratch=[pltpu.VMEM((2 * FPAD, 2 * ROWS), BF)] * 2,
+        scratch=[pltpu.VMEM((2 * FPAD, 2 * ROWS), BF)] * 2 + [pltpu.VMEM((4, ROWS, 2 * FPAD), BF)],
         limit=BIG,
         grid=(4,),
-        out_specs=[
-            pl.BlockSpec((6 * FPAD, PAIR), lambda i: (0, i)),
-            pl.BlockSpec((2, ROWS, 2 * FPAD), lambda i: (0, 0, 0)),
-        ],
+        out_specs=pl.BlockSpec((6 * FPAD + ROWS, PAIR), lambda i: (0, i)),
     )(*operands)
     parts = call(
         main_kernel,
         sds((TEN * PIECE, 128)),
-        [VM, VM, AN],
+        [VM, AN],
         23 * 10**8,
         12 * 10**6,
-        scratch=[pltpu.VMEM((ROWS, D), BF), pltpu.VMEM((6 * FPAD, D), BF), pltpu.SemaphoreType.DMA((2,))],
+        scratch=[
+            pltpu.VMEM((ROWS, D), BF),
+            pltpu.VMEM((6 * FPAD, D), BF),
+            pltpu.VMEM((4, ROWS, FULL), BF),
+            pltpu.SemaphoreType.DMA((9,)),
+        ],
         limit=MID,
-    )(pieces, factors, weights)
-    home = exchange(parts, ("yl", "x"), TEN)
+    )(pieces, weights)
+    home = exchange(parts, ("x", "yl"), TEN)
     summed = call(unsort_kernel, sds((EXP * BLK, 128)), [VM], 10**9, 3 * 10**6)(home)
-    back = exchange(summed, ("z", "yh"), EXP)
+    back = exchange(summed, ("yh", "z"), EXP)
     out_t = call(combine_kernel, sds((FEAT, TOK)), [VM, VM], 10**9, 10**6)(back, target)
     return out_t.T
 

time: 129 us -> 129 us (level)
  blocking collectives: 80.7 us -> 82 us
    all_to_all x3, blocking collectives: 80.7 us -> 82 us  [exchange(): lax.all_to_all(blocks, axes, split_axis=0, concat_axis=0, tiled=True)]
    unnamed x14 -> x12, local copies, waits for them, and re-layouts: 3.65 us -> 2.47 us
where the time goes in v5:
time: 129 us; the launch traced here: 126 us
  blocking collectives  82 us (64%)
  Pallas kernels  18.9 us (15%)
  starting transfers between devices  18.2 us (14%)
  waiting for transfers between devices  4.73 us (4%)
  local copies, waits for them, and re-layouts  2.47 us (2%)
    all_to_all x3, blocking collectives, exchange(): lax.all_to_all(blocks, axes, split_axis=0, concat_axis=0, tiled=True)  82 us
    ppermute x5, starting transfers between devices, swap_core(): return lax.ppermute(a, 'core', [(0, 1), (1, 0)])  14 us
    pallas_call x1, Pallas kernels, shards(): call(stack_kernel, sds((6 * FPAD + ROWS, D)), [block] * 6 + [saved] * 4,...  7.86 us
    pallas_call x1, Pallas kernels, shards(): call(main_kernel, sds((TEN * PIECE, 128)), [VM, AN], 23 * 10 ** 8, 12 * 1...  6.03 us
    all_to_all x1, starting transfers between devices, exchange(): lax.all_to_all(blocks, axes, split_axis=0, concat_axis=0, tiled=True)  4.15 us
    all_to_all x1, waiting for transfers between devices, exchange(): lax.all_to_all(blocks, axes, split_axis=0, concat_axis=0, tiled=True)  3.48 us
    pallas_call x1, Pallas kernels, shards(): call(pack_kernel, [sds((EXP * BLK, 128)), sds((2, TOK), jnp.int32)], [VM,...  2.61 us
  transfers between devices with their start and end apart: 6, of which 2 were waited for; matrix products, arithmetic and copies ran while one was open for 0% of the time, Pallas kernels for 6%

profile of v5, /device:TPU:1, one launch (start us, length us, event | category | flops | bytes accessed | tf_op | source)
XLA Modules:
  0.0 126.3 jit_solution(11133983516396119185)
XLA Ops:
  0.0 2.6 %shard_map.82 = (bf16[1280,128]{1,0:T(8,128)(2,1)}, s32[2,128]{1,0:T(2,128)}) custom-call(bf16[448,128]{1,0:T(8,128)(2,1)} %bitcast.20, f32[2,128]{1,0:T(2,128)} %bitcast.21, s32[2,128]{1,0:T(2,128)} %bitcast.22), custom_call_target="tpu_custom_call" | custom-call | flops 1000000000 | bytes 1000000 | tf_op jit(solution)/shard_map/pallas_call | solution.py:254
  2.6 29.8 %all_to_all.20 = bf16[32,40,128]{2,1,0:T(8,128)(2,1)S(1)} all-to-all(bf16[32,40,128]{2,1,0:T(8,128)(2,1)} %bitcast.19), channel_id=1, replica_groups=mesh['z'=8,'yh'=4,'core'=2,'x'=4,'yl'=2] {'yh','z'}, dimensions={0} | all-to-all | bytes 655360 | tf_op jit(solution)/shard_map/all_to_all | solution.py:250
  32.4 0.4 shard_map.83
  32.8 0.0 copy-start
  32.8 1.4 %copy-done = bf16[8960,128]{1,0:T(8,128)(2,1)} copy-done((bf16[8960,128]{1,0:T(8,128)(2,1)}, bf16[8960,128]{1,0:T(8,128)(2,1)S(1)}, u32[]{:S(2)}) %copy-start) | copy-done | bytes 2293784
  34.2 0.0 copy-start.2
  34.2 4.1 %all-to-all-start.1 = ((bf16[8,1120,128]{2,1,0:T(8,128)(2,1)}), bf16[8,1120,128]{2,1,0:T(8,128)(2,1)S(1)}, u32[]{:S(2)}, u32[]{:S(2)}) async-start(bf16[8,1120,128]{2,1,0:T(8,128)(2,1)} %bitcast.14), calls=%async_computation.1 | async-start | bytes 4587520 | tf_op jit(solution)/shard_map/all_to_all | solution.py:250
  38.3 5.4 %collective-permute-start.1 = (bf16[152,3584]{1,0:T(8,128)(2,1)}, bf16[152,3584]{1,0:T(8,128)(2,1)S(1)}, u32[]{:S(2)}, u32[]{:S(2)}) collective-permute-start(bf16[152,3584]{1,0:T(8,128)(2,1)} %wg0.1), channel_id=1, source_target_pairs={{0,8},{8,0},{1,9},{9,1},{2,10},{10,2},{3,11},{11,3},{4,12},{12,4},... | collective-permute-start | bytes 3268616 | tf_op jit(solution)/shard_map/ppermute | solution.py:245
  43.7 1.9 %collective-permute-start.2 = (bf16[152,3584]{1,0:T(8,128)(2,1)}, bf16[152,3584]{1,0:T(8,128)(2,1)}, u32[]{:S(2)}, u32[]{:S(2)}) collective-permute-start(bf16[152,3584]{1,0:T(8,128)(2,1)} %wu0.1), channel_id=1, source_target_pairs={{0,8},{8,0},{1,9},{9,1},{2,10},{10,2},{3,11},{11,3},{4,12},{12,4},... | collective-permute-start | bytes 3268616 | tf_op jit(solution)/shard_map/ppermute | solution.py:245
  45.6 0.0 copy-done.2
  45.6 2.4 %collective-permute-start = (bf16[152,3584]{1,0:T(8,128)(2,1)S(1)}, bf16[152,3584]{1,0:T(8,128)(2,1)}, u32[]{:S(2)}, u32[]{:S(2)}) collective-permute-start(bf16[152,3584]{1,0:T(8,128)(2,1)S(1)} %copy-done.2), channel_id=1, source_target_pairs={{0,8},{8,0},{1,9},{9,1},{2,10},{10,2},{3,11},{11,3},{4,12},{12,4},... | collective-permute-start | bytes 3268616 | tf_op jit(solution)/shard_map/ppermute | solution.py:245
  48.0 1.9 %collective-permute-start.3 = (bf16[152,640]{1,0:T(8,128)(2,1)}, bf16[152,640]{1,0:T(8,128)(2,1)S(1)}, u32[]{:S(2)}, u32[]{:S(2)}) collective-permute-start(bf16[152,640]{1,0:T(8,128)(2,1)} %sg0.1), channel_id=1, source_target_pairs={{0,8},{8,0},{1,9},{9,1},{2,10},{10,2},{3,11},{11,3},{4,12},{12,4},... | collective-permute-start | bytes 583688 | tf_op jit(solution)/shard_map/ppermute | solution.py:245
  50.0 2.4 %collective-permute-start.4 = (bf16[152,640]{1,0:T(8,128)(2,1)}, bf16[152,640]{1,0:T(8,128)(2,1)S(1)}, u32[]{:S(2)}, u32[]{:S(2)}) collective-permute-start(bf16[152,640]{1,0:T(8,128)(2,1)} %su0.1), channel_id=1, source_target_pairs={{0,8},{8,0},{1,9},{9,1},{2,10},{10,2},{3,11},{11,3},{4,12},{12,4},... | collective-permute-start | bytes 583688 | tf_op jit(solution)/shard_map/ppermute | solution.py:245
  52.4 0.0 collective-permute-done.3.sg1
  52.4 0.0 copy-start.4
  52.4 1.2 collective-permute-done.4.su1
  53.6 0.0 copy-start.5
  53.7 0.0 collective-permute-done.1.wg1
  53.7 0.0 copy-start.3
  53.7 0.0 collective-permute-done.2.wu1
  53.7 0.0 collective-permute-done.wd1
  53.7 0.0 copy-done.4
  53.7 0.6 copy-done.5
  54.3 0.5 copy-done.3
  54.8 7.9 %shard_map.84.w_hbm = bf16[1280,3584]{1,0:T(8,128)(2,1)} custom-call(bf16[152,3584]{1,0:T(8,128)(2,1)} %wd0.1, bf16[152,3584]{1,0:T(8,128)(2,1)} %collective-permute-done.wd1, bf16[152,3584]{1,0:T(8,128)(2,1)} %wg0.1, bf16[152,3584]{1,0:T(8,128)(2,1)} %copy-done.3, bf16[152,3584]{1,0:T(8,128)(2,1)} %wu0.1, bf16[152,3584]{1,0:T(8,128)(2,1)} %collective-permute-done.2.wu1, ...), custom_call_target="tpu_custom_call" | custom-call | flops 500000000 | bytes 16000000 | tf_op jit(solution)/shard_map/pallas_call | solution.py:271
  62.6 3.5 %all-to-all-done.1 = bf16[8,1120,128]{2,1,0:T(8,128)(2,1)S(1)} async-done(((bf16[8,1120,128]{2,1,0:T(8,128)(2,1)}), bf16[8,1120,128]{2,1,0:T(8,128)(2,1)S(1)}, u32[]{:S(2)}, u32[]{:S(2)}) %all-to-all-start.1) | async-done | bytes 2293792 | tf_op jit(solution)/shard_map/all_to_all | solution.py:250
  66.1 6.0 %shard_map.85 = bf16[8960,128]{1,0:T(8,128)(2,1)S(1)} custom-call(bf16[8960,128]{1,0:T(8,128)(2,1)S(1)} %bitcast.12, bf16[1280,3584]{1,0:T(8,128)(2,1)} %shard_map.84.w_hbm), custom_call_target="tpu_custom_call" | custom-call | flops 2300000000 | bytes 12000000 | tf_op jit(solution)/shard_map/pallas_call | solution.py:282
  72.2 32.6 %all_to_all.21 = bf16[8,1120,128]{2,1,0:T(8,128)(2,1)S(1)} all-to-all(bf16[8,1120,128]{2,1,0:T(8,128)(2,1)S(1)} %bitcast.13), channel_id=1, replica_groups=mesh['z'=8,'yh'=4,'core'=2,'x'=4,'yl'=2] {'x','yl'}, dimensions={0} | all-to-all | bytes 4587520 | tf_op jit(solution)/shard_map/all_to_all | solution.py:250
  104.8 0.0 copy-start.1
  104.8 0.9 shard_map.86
  105.6 19.6 %all_to_all.22 = bf16[32,40,128]{2,1,0:T(8,128)(2,1)S(1)} all-to-all(bf16[32,40,128]{2,1,0:T(8,128)(2,1)S(1)} %bitcast.18), channel_id=1, replica_groups=mesh['z'=8,'yh'=4,'core'=2,'x'=4,'yl'=2] {'yh','z'}, dimensions={0} | all-to-all | bytes 655360 | tf_op jit(solution)/shard_map/all_to_all | solution.py:250
  125.2 0.0 copy-done.1
  125.2 1.1 shard_map.87
Async XLA Ops:
  32.8 1.4 %copy-start = (bf16[8960,128]{1,0:T(8,128)(2,1)}, bf16[8960,128]{1,0:T(8,128)(2,1)S(1)}, u32[]{:S(2)}) copy-start(bf16[8960,128]{1,0:T(8,128)(2,1)S(1)} %shard_map.83) | copy-start | bytes 6881284
  34.2 11.4 %copy-start.2 = (bf16[152,3584]{1,0:T(8,128)(2,1)S(1)}, bf16[152,3584]{1,0:T(8,128)(2,1)}, u32[]{:S(2)}) copy-start(bf16[152,3584]{1,0:T(8,128)(2,1)} %wd0.1) | copy-start | bytes 3268612
  34.2 31.9 %all-to-all-start.1 = ((bf16[8,1120,128]{2,1,0:T(8,128)(2,1)}), bf16[8,1120,128]{2,1,0:T(8,128)(2,1)S(1)}, u32[]{:S(2)}, u32[]{:S(2)}) async-start(bf16[8,1120,128]{2,1,0:T(8,128)(2,1)} %bitcast.14), calls=%async_computation.1 | async-start | bytes 4587520 | tf_op jit(solution)/shard_map/all_to_all | solution.py:250
  38.3 15.3 %collective-permute-start.1 = (bf16[152,3584]{1,0:T(8,128)(2,1)}, bf16[152,3584]{1,0:T(8,128)(2,1)S(1)}, u32[]{:S(2)}, u32[]{:S(2)}) collective-permute-start(bf16[152,3584]{1,0:T(8,128)(2,1)} %wg0.1), channel_id=1, source_target_pairs={{0,8},{8,0},{1,9},{9,1},{2,10},{10,2},{3,11},{11,3},{4,12},{12,4},... | collective-permute-start | bytes 3268616 | tf_op jit(solution)/shard_map/ppermute | solution.py:245
  43.7 10.0 %collective-permute-start.2 = (bf16[152,3584]{1,0:T(8,128)(2,1)}, bf16[152,3584]{1,0:T(8,128)(2,1)}, u32[]{:S(2)}, u32[]{:S(2)}) collective-permute-start(bf16[152,3584]{1,0:T(8,128)(2,1)} %wu0.1), channel_id=1, source_target_pairs={{0,8},{8,0},{1,9},{9,1},{2,10},{10,2},{3,11},{11,3},{4,12},{12,4},... | collective-permute-start | bytes 3268616 | tf_op jit(solution)/shard_map/ppermute | solution.py:245
  45.6 8.0 %collective-permute-start = (bf16[152,3584]{1,0:T(8,128)(2,1)S(1)}, bf16[152,3584]{1,0:T(8,128)(2,1)}, u32[]{:S(2)}, u32[]{:S(2)}) collective-permute-start(bf16[152,3584]{1,0:T(8,128)(2,1)S(1)} %copy-done.2), channel_id=1, source_target_pairs={{0,8},{8,0},{1,9},{9,1},{2,10},{10,2},{3,11},{11,3},{4,12},{12,4},... | collective-permute-start | bytes 3268616 | tf_op jit(solution)/shard_map/ppermute | solution.py:245
  48.0 4.3 %collective-permute-start.3 = (bf16[152,640]{1,0:T(8,128)(2,1)}, bf16[152,640]{1,0:T(8,128)(2,1)S(1)}, u32[]{:S(2)}, u32[]{:S(2)}) collective-permute-start(bf16[152,640]{1,0:T(8,128)(2,1)} %sg0.1), channel_id=1, source_target_pairs={{0,8},{8,0},{1,9},{9,1},{2,10},{10,2},{3,11},{11,3},{4,12},{12,4},... | collective-permute-start | bytes 583688 | tf_op jit(solution)/shard_map/ppermute | solution.py:245
  50.0 3.7 %collective-permute-start.4 = (bf16[152,640]{1,0:T(8,128)(2,1)}, bf16[152,640]{1,0:T(8,128)(2,1)S(1)}, u32[]{:S(2)}, u32[]{:S(2)}) collective-permute-start(bf16[152,640]{1,0:T(8,128)(2,1)} %su0.1), channel_id=1, source_target_pairs={{0,8},{8,0},{1,9},{9,1},{2,10},{10,2},{3,11},{11,3},{4,12},{12,4},... | collective-permute-start | bytes 583688 | tf_op jit(solution)/shard_map/ppermute | solution.py:245
  52.4 1.3 %copy-start.4 = (bf16[152,640]{1,0:T(8,128)(2,1)}, bf16[152,640]{1,0:T(8,128)(2,1)S(1)}, u32[]{:S(2)}) copy-start(bf16[152,640]{1,0:T(8,128)(2,1)S(1)} %collective-permute-done.3.sg1) | copy-start | bytes 583684
  53.6 0.7 copy-start.5
  53.7 1.1 copy-start.3
  104.8 20.4 %copy-start.1 = (s32[2,128]{1,0:T(2,128)S(1)}, s32[2,128]{1,0:T(2,128)}, u32[]{:S(2)}) copy-start(s32[2,128]{1,0:T(2,128)} %get-tuple-element.8.tgt_ref) | copy-start | bytes 3076

commit v6 on v5

--- a/solution.py
+++ b/solution.py
@@ -40,8 +40,7 @@
 
 
 def block_ids(rows=BLK):
-    p = lax.broadcasted_iota(jnp.int32, (EXP, rows, TOK), 0).reshape(EXP * rows, TOK)
-    e = 4 * (p & 7) + (p >> 3)
+    e = lax.broadcasted_iota(jnp.int32, (EXP, rows, TOK), 0).reshape(EXP * rows, TOK)
     k = lax.broadcasted_iota(jnp.int32, (EXP, rows, TOK), 1).reshape(EXP * rows, TOK)
     return e, k
 
@@ -125,9 +124,7 @@
         col = lax.broadcasted_iota(jnp.int32, (ROWS, 2 * ROWS), 1)
         h = (r >= HROWS).astype(jnp.int32)
         q = r - HROWS * h
-        p = (q * 205) >> 10
-        source = 4 * (p & 7) + (p >> 3)
-        pick = (col == 2 * CAP * source + (q - HALF * p) + HALF * h + CAP * core).astype(F32).astype(BF)
+        pick = (col == 15 * ((q * 205) >> 10) + q + HALF * h + CAP * core).astype(F32).astype(BF)
         g = nt(pick, sg_ref[...])
         u = nt(pick, su_ref[...])
         sig = 1.0 / (1.0 + jnp.exp(-g))
@@ -141,7 +138,10 @@
 
 def main_kernel(in_ref, w_hbm, out_ref, r_ref, w_ref, f_ref, sems):
     down, rest = 2 * FPAD, 4 * FPAD
-    pairs = [(w_hbm.at[pl.ds(0, down), :], w_ref.at[pl.ds(0, down), :])]
+    pairs = []
+    for i in range(4):
+        at = (pl.ds(0, down), pl.ds(i * PAIR, PAIR))
+        pairs.append((w_hbm.at[at], w_ref.at[at]))
     for i in range(4):
         pairs.append((w_hbm.at[pl.ds(down + rest, ROWS), pl.ds(i * PAIR, FULL)], f_ref.at[i]))
     for i in range(4):
@@ -150,6 +150,7 @@
     copies = [pltpu.make_async_copy(src, dst, sems.at[i]) for i, (src, dst) in enumerate(pairs)]
     for copy in copies:
         copy.start()
+    hidden = None
     for i in range(4):
         base, even, odd = i * PAIR, i * PIECE, (4 + i) * PIECE
         for j in range(3):
@@ -160,15 +161,16 @@
         oh = in_ref[odd + 3 * ROWS : odd + PIECE, :]
         r_ref[0:HROWS, base + FULL : base + 512] = jnp.concatenate([eh[:, :64], oh[:, :64]], axis=1)
         r_ref[HROWS:ROWS, base + FULL : base + 512] = jnp.concatenate([eh[:, 64:], oh[:, 64:]], axis=1)
-    copies[0].wait()
-    hidden = nt(r_ref[...], w_ref[0:down, :])
-    for copy in copies[1:5]:
+        copies[i].wait()
+        term = nt(r_ref[:, base : base + PAIR], w_ref[0:down, base : base + PAIR])
+        hidden = term if hidden is None else hidden + term
+    for copy in copies[4:8]:
         copy.wait()
     part = lambda i: f_ref[i, :, 0:down].astype(F32)
     grads = jnp.concatenate([hidden * (part(0) + part(1)), hidden * (part(2) + part(3))], axis=1).astype(BF)
     for i in range(4):
         base, even, odd = i * PAIR, 2 * i * PIECE, (2 * i + 1) * PIECE
-        copies[5 + i].wait()
+        copies[8 + i].wait()
         acc = jnp.dot(grads, w_ref[down:, base : base + PAIR], preferred_element_type=F32).astype(BF)
         for j in range(3):
             out_ref[even + j * ROWS : even + (j + 1) * ROWS, :] = acc[:, 128 * j : 128 * (j + 1)]
@@ -259,7 +261,7 @@
         10**6,
         limit=BIG,
     )(out_grad.T, gate_probs.T, expert_ids.T)
-    got = exchange(packed, ("yh", "z"), EXP)
+    got = exchange(packed, ("z", "yh"), EXP)
     spread = call(sort_kernel, sds((TEN * PIECE, 128)), [VM], 10**9, 3 * 10**6)(got)
     pieces = exchange(spread, ("yl", "x"), TEN)
 
@@ -289,13 +291,13 @@
             pltpu.VMEM((ROWS, D), BF),
             pltpu.VMEM((6 * FPAD, D), BF),
             pltpu.VMEM((4, ROWS, FULL), BF),
-            pltpu.SemaphoreType.DMA((9,)),
+            pltpu.SemaphoreType.DMA((12,)),
         ],
         limit=MID,
     )(pieces, weights)
     home = exchange(parts, ("x", "yl"), TEN)
     summed = call(unsort_kernel, sds((EXP * BLK, 128)), [VM], 10**9, 3 * 10**6)(home)
-    back = exchange(summed, ("yh", "z"), EXP)
+    back = exchange(summed, ("z", "yh"), EXP)
     out_t = call(combine_kernel, sds((FEAT, TOK)), [VM, VM], 10**9, 10**6)(back, target)
     return out_t.T
 

time: 129 us -> 129 us (level)
  the two profiles are of different devices: /device:TPU:1 before, /device:TPU:16 now
where the time goes in v6:
time: 129 us
  blocking collectives  83.7 us (65%)
  Pallas kernels  19.2 us (15%)
  starting transfers between devices  15 us (12%)
  waiting for transfers between devices  8.14 us (6%)
  local copies, waits for them, and re-layouts  2.47 us (2%)
    all_to_all x3, blocking collectives, exchange(): lax.all_to_all(blocks, axes, split_axis=0, concat_axis=0, tiled=True)  83.7 us
    ppermute x5, starting transfers between devices, swap_core(): return lax.ppermute(a, 'core', [(0, 1), (1, 0)])  10.6 us
    pallas_call x1, Pallas kernels, shards(): call(stack_kernel, sds((6 * FPAD + ROWS, D)), [block] * 6 + [saved] * 4,...  7.85 us
    all_to_all x1, waiting for transfers between devices, exchange(): lax.all_to_all(blocks, axes, split_axis=0, concat_axis=0, tiled=True)  6.54 us
    pallas_call x1, Pallas kernels, shards(): call(main_kernel, sds((TEN * PIECE, 128)), [VM, AN], 23 * 10 ** 8, 12 * 1...  6.33 us
    all_to_all x1, starting transfers between devices, exchange(): lax.all_to_all(blocks, axes, split_axis=0, concat_axis=0, tiled=True)  4.45 us
    pallas_call x1, Pallas kernels, shards(): call(pack_kernel, [sds((EXP * BLK, 128)), sds((2, TOK), jnp.int32)], [VM,...  2.62 us
  transfers between devices with their start and end apart: 6, of which 2 were waited for; matrix products, arithmetic and copies ran while one was open for 0% of the time, Pallas kernels for 6%

profile of v6, /device:TPU:16, one launch (start us, length us, event | category | flops | bytes accessed | tf_op | source)
XLA Modules:
  0.0 128.6 jit_solution(1246453150067606473)
XLA Ops:
  0.0 2.6 %shard_map.82 = (bf16[1280,128]{1,0:T(8,128)(2,1)}, s32[2,128]{1,0:T(2,128)}) custom-call(bf16[448,128]{1,0:T(8,128)(2,1)} %bitcast.20, f32[2,128]{1,0:T(2,128)} %bitcast.21, s32[2,128]{1,0:T(2,128)} %bitcast.22), custom_call_target="tpu_custom_call" | custom-call | flops 1000000000 | bytes 1000000 | tf_op jit(solution)/shard_map/pallas_call | solution.py:256
  2.6 31.3 %all_to_all.20 = bf16[32,40,128]{2,1,0:T(8,128)(2,1)S(1)} all-to-all(bf16[32,40,128]{2,1,0:T(8,128)(2,1)} %bitcast.19), channel_id=1, replica_groups=mesh['z'=8,'yh'=4,'core'=2,'x'=4,'yl'=2] {'z','yh'}, dimensions={0} | all-to-all | bytes 655360 | tf_op jit(solution)/shard_map/all_to_all | solution.py:252
  33.9 0.4 shard_map.83
  34.4 0.0 copy-start
  34.4 1.4 %copy-done = bf16[8960,128]{1,0:T(8,128)(2,1)} copy-done((bf16[8960,128]{1,0:T(8,128)(2,1)}, bf16[8960,128]{1,0:T(8,128)(2,1)S(1)}, u32[]{:S(2)}) %copy-start) | copy-done | bytes 2293784
  35.7 0.0 copy-start.2
  35.7 4.4 %all-to-all-start.1 = ((bf16[8,1120,128]{2,1,0:T(8,128)(2,1)}), bf16[8,1120,128]{2,1,0:T(8,128)(2,1)S(1)}, u32[]{:S(2)}, u32[]{:S(2)}) async-start(bf16[8,1120,128]{2,1,0:T(8,128)(2,1)} %bitcast.14), calls=%async_computation.1 | async-start | bytes 4587520 | tf_op jit(solution)/shard_map/all_to_all | solution.py:252
  40.2 1.9 %collective-permute-start.1 = (bf16[152,3584]{1,0:T(8,128)(2,1)}, bf16[152,3584]{1,0:T(8,128)(2,1)S(1)}, u32[]{:S(2)}, u32[]{:S(2)}) collective-permute-start(bf16[152,3584]{1,0:T(8,128)(2,1)} %wg0.1), channel_id=1, source_target_pairs={{0,8},{8,0},{1,9},{9,1},{2,10},{10,2},{3,11},{11,3},{4,12},{12,4},... | collective-permute-start | bytes 3268616 | tf_op jit(solution)/shard_map/ppermute | solution.py:247
  42.1 2.4 %collective-permute-start.2 = (bf16[152,3584]{1,0:T(8,128)(2,1)}, bf16[152,3584]{1,0:T(8,128)(2,1)}, u32[]{:S(2)}, u32[]{:S(2)}) collective-permute-start(bf16[152,3584]{1,0:T(8,128)(2,1)} %wu0.1), channel_id=1, source_target_pairs={{0,8},{8,0},{1,9},{9,1},{2,10},{10,2},{3,11},{11,3},{4,12},{12,4},... | collective-permute-start | bytes 3268616 | tf_op jit(solution)/shard_map/ppermute | solution.py:247
  44.5 0.0 copy-done.2
  44.5 1.9 %collective-permute-start = (bf16[152,3584]{1,0:T(8,128)(2,1)S(1)}, bf16[152,3584]{1,0:T(8,128)(2,1)}, u32[]{:S(2)}, u32[]{:S(2)}) collective-permute-start(bf16[152,3584]{1,0:T(8,128)(2,1)S(1)} %copy-done.2), channel_id=1, source_target_pairs={{0,8},{8,0},{1,9},{9,1},{2,10},{10,2},{3,11},{11,3},{4,12},{12,4},... | collective-permute-start | bytes 3268616 | tf_op jit(solution)/shard_map/ppermute | solution.py:247
  46.4 2.4 %collective-permute-start.3 = (bf16[152,640]{1,0:T(8,128)(2,1)}, bf16[152,640]{1,0:T(8,128)(2,1)S(1)}, u32[]{:S(2)}, u32[]{:S(2)}) collective-permute-start(bf16[152,640]{1,0:T(8,128)(2,1)} %sg0.1), channel_id=1, source_target_pairs={{0,8},{8,0},{1,9},{9,1},{2,10},{10,2},{3,11},{11,3},{4,12},{12,4},... | collective-permute-start | bytes 583688 | tf_op jit(solution)/shard_map/ppermute | solution.py:247
  48.9 1.9 %collective-permute-start.4 = (bf16[152,640]{1,0:T(8,128)(2,1)}, bf16[152,640]{1,0:T(8,128)(2,1)S(1)}, u32[]{:S(2)}, u32[]{:S(2)}) collective-permute-start(bf16[152,640]{1,0:T(8,128)(2,1)} %su0.1), channel_id=1, source_target_pairs={{0,8},{8,0},{1,9},{9,1},{2,10},{10,2},{3,11},{11,3},{4,12},{12,4},... | collective-permute-start | bytes 583688 | tf_op jit(solution)/shard_map/ppermute | solution.py:247
  50.8 0.0 collective-permute-done.3.sg1
  50.8 0.0 copy-start.4
  50.8 1.6 %collective-permute-done.4.su1 = bf16[152,640]{1,0:T(8,128)(2,1)S(1)} collective-permute-done((bf16[152,640]{1,0:T(8,128)(2,1)}, bf16[152,640]{1,0:T(8,128)(2,1)S(1)}, u32[]{:S(2)}, u32[]{:S(2)}) %collective-permute-start.4) | collective-permute-done | bytes 194592 | tf_op jit(solution)/shard_map/ppermute | solution.py:247
  52.4 0.0 copy-start.5
  52.4 0.0 collective-permute-done.1.wg1
  52.4 0.0 copy-start.3
  52.4 0.0 collective-permute-done.2.wu1
  52.4 0.0 collective-permute-done.wd1
  52.4 0.0 copy-done.4
  52.4 0.6 copy-done.5
  53.1 0.5 copy-done.3
  53.5 7.8 %shard_map.84.w_hbm = bf16[1280,3584]{1,0:T(8,128)(2,1)} custom-call(bf16[152,3584]{1,0:T(8,128)(2,1)} %wd0.1, bf16[152,3584]{1,0:T(8,128)(2,1)} %collective-permute-done.wd1, bf16[152,3584]{1,0:T(8,128)(2,1)} %wg0.1, bf16[152,3584]{1,0:T(8,128)(2,1)} %copy-done.3, bf16[152,3584]{1,0:T(8,128)(2,1)} %wu0.1, bf16[152,3584]{1,0:T(8,128)(2,1)} %collective-permute-done.2.wu1, ...), custom_call_target="tpu_custom_call" | custom-call | flops 500000000 | bytes 16000000 | tf_op jit(solution)/shard_map/pallas_call | solution.py:273
  61.4 6.5 %all-to-all-done.1 = bf16[8,1120,128]{2,1,0:T(8,128)(2,1)S(1)} async-done(((bf16[8,1120,128]{2,1,0:T(8,128)(2,1)}), bf16[8,1120,128]{2,1,0:T(8,128)(2,1)S(1)}, u32[]{:S(2)}, u32[]{:S(2)}) %all-to-all-start.1) | async-done | bytes 2293792 | tf_op jit(solution)/shard_map/all_to_all | solution.py:252
  67.9 6.3 %shard_map.85 = bf16[8960,128]{1,0:T(8,128)(2,1)S(1)} custom-call(bf16[8960,128]{1,0:T(8,128)(2,1)S(1)} %bitcast.12, bf16[1280,3584]{1,0:T(8,128)(2,1)} %shard_map.84.w_hbm), custom_call_target="tpu_custom_call" | custom-call | flops 2300000000 | bytes 12000000 | tf_op jit(solution)/shard_map/pallas_call | solution.py:284
  74.3 33.0 %all_to_all.21 = bf16[8,1120,128]{2,1,0:T(8,128)(2,1)S(1)} all-to-all(bf16[8,1120,128]{2,1,0:T(8,128)(2,1)S(1)} %bitcast.13), channel_id=1, replica_groups=mesh['z'=8,'yh'=4,'core'=2,'x'=4,'yl'=2] {'x','yl'}, dimensions={0} | all-to-all | bytes 4587520 | tf_op jit(solution)/shard_map/all_to_all | solution.py:252
  107.2 0.0 copy-start.1
  107.2 0.9 shard_map.86
  108.1 19.4 %all_to_all.22 = bf16[32,40,128]{2,1,0:T(8,128)(2,1)S(1)} all-to-all(bf16[32,40,128]{2,1,0:T(8,128)(2,1)S(1)} %bitcast.18), channel_id=1, replica_groups=mesh['z'=8,'yh'=4,'core'=2,'x'=4,'yl'=2] {'z','yh'}, dimensions={0} | all-to-all | bytes 655360 | tf_op jit(solution)/shard_map/all_to_all | solution.py:252
  127.5 0.0 copy-done.1
  127.5 1.1 shard_map.87
Async XLA Ops:
  34.4 1.4 %copy-start = (bf16[8960,128]{1,0:T(8,128)(2,1)}, bf16[8960,128]{1,0:T(8,128)(2,1)S(1)}, u32[]{:S(2)}) copy-start(bf16[8960,128]{1,0:T(8,128)(2,1)S(1)} %shard_map.83) | copy-start | bytes 6881284
  35.7 8.8 %copy-start.2 = (bf16[152,3584]{1,0:T(8,128)(2,1)S(1)}, bf16[152,3584]{1,0:T(8,128)(2,1)}, u32[]{:S(2)}) copy-start(bf16[152,3584]{1,0:T(8,128)(2,1)} %wd0.1) | copy-start | bytes 3268612
  35.7 32.2 %all-to-all-start.1 = ((bf16[8,1120,128]{2,1,0:T(8,128)(2,1)}), bf16[8,1120,128]{2,1,0:T(8,128)(2,1)S(1)}, u32[]{:S(2)}, u32[]{:S(2)}) async-start(bf16[8,1120,128]{2,1,0:T(8,128)(2,1)} %bitcast.14), calls=%async_computation.1 | async-start | bytes 4587520 | tf_op jit(solution)/shard_map/all_to_all | solution.py:252
  40.2 12.2 %collective-permute-start.1 = (bf16[152,3584]{1,0:T(8,128)(2,1)}, bf16[152,3584]{1,0:T(8,128)(2,1)S(1)}, u32[]{:S(2)}, u32[]{:S(2)}) collective-permute-start(bf16[152,3584]{1,0:T(8,128)(2,1)} %wg0.1), channel_id=1, source_target_pairs={{0,8},{8,0},{1,9},{9,1},{2,10},{10,2},{3,11},{11,3},{4,12},{12,4},... | collective-permute-start | bytes 3268616 | tf_op jit(solution)/shard_map/ppermute | solution.py:247
  42.1 10.3 %collective-permute-start.2 = (bf16[152,3584]{1,0:T(8,128)(2,1)}, bf16[152,3584]{1,0:T(8,128)(2,1)}, u32[]{:S(2)}, u32[]{:S(2)}) collective-permute-start(bf16[152,3584]{1,0:T(8,128)(2,1)} %wu0.1), channel_id=1, source_target_pairs={{0,8},{8,0},{1,9},{9,1},{2,10},{10,2},{3,11},{11,3},{4,12},{12,4},... | collective-permute-start | bytes 3268616 | tf_op jit(solution)/shard_map/ppermute | solution.py:247
  44.5 7.9 %collective-permute-start = (bf16[152,3584]{1,0:T(8,128)(2,1)S(1)}, bf16[152,3584]{1,0:T(8,128)(2,1)}, u32[]{:S(2)}, u32[]{:S(2)}) collective-permute-start(bf16[152,3584]{1,0:T(8,128)(2,1)S(1)} %copy-done.2), channel_id=1, source_target_pairs={{0,8},{8,0},{1,9},{9,1},{2,10},{10,2},{3,11},{11,3},{4,12},{12,4},... | collective-permute-start | bytes 3268616 | tf_op jit(solution)/shard_map/ppermute | solution.py:247
  46.4 4.3 %collective-permute-start.3 = (bf16[152,640]{1,0:T(8,128)(2,1)}, bf16[152,640]{1,0:T(8,128)(2,1)S(1)}, u32[]{:S(2)}, u32[]{:S(2)}) collective-permute-start(bf16[152,640]{1,0:T(8,128)(2,1)} %sg0.1), channel_id=1, source_target_pairs={{0,8},{8,0},{1,9},{9,1},{2,10},{10,2},{3,11},{11,3},{4,12},{12,4},... | collective-permute-start | bytes 583688 | tf_op jit(solution)/shard_map/ppermute | solution.py:247
  48.9 3.5 %collective-permute-start.4 = (bf16[152,640]{1,0:T(8,128)(2,1)}, bf16[152,640]{1,0:T(8,128)(2,1)S(1)}, u32[]{:S(2)}, u32[]{:S(2)}) collective-permute-start(bf16[152,640]{1,0:T(8,128)(2,1)} %su0.1), channel_id=1, source_target_pairs={{0,8},{8,0},{1,9},{9,1},{2,10},{10,2},{3,11},{11,3},{4,12},{12,4},... | collective-permute-start | bytes 583688 | tf_op jit(solution)/shard_map/ppermute | solution.py:247
  50.8 1.6 %copy-start.4 = (bf16[152,640]{1,0:T(8,128)(2,1)}, bf16[152,640]{1,0:T(8,128)(2,1)S(1)}, u32[]{:S(2)}) copy-start(bf16[152,640]{1,0:T(8,128)(2,1)S(1)} %collective-permute-done.3.sg1) | copy-start | bytes 583684
  52.4 0.7 copy-start.5
  52.4 1.1 copy-start.3
  107.2 20.3 %copy-start.1 = (s32[2,128]{1,0:T(2,128)S(1)}, s32[2,128]{1,0:T(2,128)}, u32[]{:S(2)}) copy-start(s32[2,128]{1,0:T(2,128)} %get-tuple-element.8.tgt_ref) | copy-start | bytes 3076

commit v7 on v5

--- a/solution.py
+++ b/solution.py
@@ -40,8 +40,7 @@
 
 
 def block_ids(rows=BLK):
-    p = lax.broadcasted_iota(jnp.int32, (EXP, rows, TOK), 0).reshape(EXP * rows, TOK)
-    e = 4 * (p & 7) + (p >> 3)
+    e = lax.broadcasted_iota(jnp.int32, (EXP, rows, TOK), 0).reshape(EXP * rows, TOK)
     k = lax.broadcasted_iota(jnp.int32, (EXP, rows, TOK), 1).reshape(EXP * rows, TOK)
     return e, k
 
@@ -125,9 +124,7 @@
         col = lax.broadcasted_iota(jnp.int32, (ROWS, 2 * ROWS), 1)
         h = (r >= HROWS).astype(jnp.int32)
         q = r - HROWS * h
-        p = (q * 205) >> 10
-        source = 4 * (p & 7) + (p >> 3)
-        pick = (col == 2 * CAP * source + (q - HALF * p) + HALF * h + CAP * core).astype(F32).astype(BF)
+        pick = (col == 15 * ((q * 205) >> 10) + q + HALF * h + CAP * core).astype(F32).astype(BF)
         g = nt(pick, sg_ref[...])
         u = nt(pick, su_ref[...])
         sig = 1.0 / (1.0 + jnp.exp(-g))
@@ -151,7 +148,7 @@
     for copy in copies:
         copy.start()
     for i in range(4):
-        base, even, odd = i * PAIR, i * PIECE, (4 + i) * PIECE
+        base, even, odd = i * PAIR, 2 * i * PIECE, (2 * i + 1) * PIECE
         for j in range(3):
             r_ref[:, base + 128 * j : base + 128 * (j + 1)] = in_ref[even + j * ROWS : even + (j + 1) * ROWS, :]
             at = base + 512 + 128 * j
@@ -259,9 +256,9 @@
         10**6,
         limit=BIG,
     )(out_grad.T, gate_probs.T, expert_ids.T)
-    got = exchange(packed, ("yh", "z"), EXP)
+    got = exchange(packed, ("z", "yh"), EXP)
     spread = call(sort_kernel, sds((TEN * PIECE, 128)), [VM], 10**9, 3 * 10**6)(got)
-    pieces = exchange(spread, ("yl", "x"), TEN)
+    pieces = exchange(spread, ("x", "yl"), TEN)
 
     operands = []
     for a in (w_down, w_gate, w_up, saved_gate, saved_up):
@@ -295,7 +292,7 @@
     )(pieces, weights)
     home = exchange(parts, ("x", "yl"), TEN)
     summed = call(unsort_kernel, sds((EXP * BLK, 128)), [VM], 10**9, 3 * 10**6)(home)
-    back = exchange(summed, ("yh", "z"), EXP)
+    back = exchange(summed, ("z", "yh"), EXP)
     out_t = call(combine_kernel, sds((FEAT, TOK)), [VM, VM], 10**9, 10**6)(back, target)
     return out_t.T
 

time: 129 us -> 129 us (level)
  the two profiles are of different devices: /device:TPU:1 before, /device:TPU:16 now
where the time goes in v7:
time: 129 us; the launch traced here: 128 us
  blocking collectives  82.7 us (64%)
  Pallas kernels  18.9 us (15%)
  starting transfers between devices  15 us (12%)
  waiting for transfers between devices  9.09 us (7%)
  local copies, waits for them, and re-layouts  2.47 us (2%)
    all_to_all x3, blocking collectives, exchange(): lax.all_to_all(blocks, axes, split_axis=0, concat_axis=0, tiled=True)  82.7 us
    ppermute x5, starting transfers between devices, swap_core(): return lax.ppermute(a, 'core', [(0, 1), (1, 0)])  10.6 us
    pallas_call x1, Pallas kernels, shards(): call(stack_kernel, sds((6 * FPAD + ROWS, D)), [block] * 6 + [saved] * 4,...  7.85 us
    all_to_all x1, waiting for transfers between devices, exchange(): lax.all_to_all(blocks, axes, split_axis=0, concat_axis=0, tiled=True)  7.48 us
    pallas_call x1, Pallas kernels, shards(): call(main_kernel, sds((TEN * PIECE, 128)), [VM, AN], 23 * 10 ** 8, 12 * 1...  6.03 us
    all_to_all x1, starting transfers between devices, exchange(): lax.all_to_all(blocks, axes, split_axis=0, concat_axis=0, tiled=True)  4.45 us
    pallas_call x1, Pallas kernels, shards(): call(pack_kernel, [sds((EXP * BLK, 128)), sds((2, TOK), jnp.int32)], [VM,...  2.62 us
  transfers between devices with their start and end apart: 6, of which 2 were waited for; matrix products, arithmetic and copies ran while one was open for 0% of the time, Pallas kernels for 6%

profile of v7, /device:TPU:16, one launch (start us, length us, event | category | flops | bytes accessed | tf_op | source)
XLA Modules:
  0.0 128.2 jit_solution(10429624221054349557)
XLA Ops:
  0.0 2.6 %shard_map.82 = (bf16[1280,128]{1,0:T(8,128)(2,1)}, s32[2,128]{1,0:T(2,128)}) custom-call(bf16[448,128]{1,0:T(8,128)(2,1)} %bitcast.20, f32[2,128]{1,0:T(2,128)} %bitcast.21, s32[2,128]{1,0:T(2,128)} %bitcast.22), custom_call_target="tpu_custom_call" | custom-call | flops 1000000000 | bytes 1000000 | tf_op jit(solution)/shard_map/pallas_call | solution.py:251
  2.6 31.3 %all_to_all.20 = bf16[32,40,128]{2,1,0:T(8,128)(2,1)S(1)} all-to-all(bf16[32,40,128]{2,1,0:T(8,128)(2,1)} %bitcast.19), channel_id=1, replica_groups=mesh['z'=8,'yh'=4,'core'=2,'x'=4,'yl'=2] {'z','yh'}, dimensions={0} | all-to-all | bytes 655360 | tf_op jit(solution)/shard_map/all_to_all | solution.py:247
  33.9 0.4 shard_map.83
  34.4 0.0 copy-start
  34.4 1.4 %copy-done = bf16[8960,128]{1,0:T(8,128)(2,1)} copy-done((bf16[8960,128]{1,0:T(8,128)(2,1)}, bf16[8960,128]{1,0:T(8,128)(2,1)S(1)}, u32[]{:S(2)}) %copy-start) | copy-done | bytes 2293784
  35.7 0.0 copy-start.2
  35.7 4.4 %all-to-all-start.1 = ((bf16[8,1120,128]{2,1,0:T(8,128)(2,1)}), bf16[8,1120,128]{2,1,0:T(8,128)(2,1)S(1)}, u32[]{:S(2)}, u32[]{:S(2)}) async-start(bf16[8,1120,128]{2,1,0:T(8,128)(2,1)} %bitcast.14), calls=%async_computation.1 | async-start | bytes 4587520 | tf_op jit(solution)/shard_map/all_to_all | solution.py:247
  40.2 1.9 %collective-permute-start.1 = (bf16[152,3584]{1,0:T(8,128)(2,1)}, bf16[152,3584]{1,0:T(8,128)(2,1)S(1)}, u32[]{:S(2)}, u32[]{:S(2)}) collective-permute-start(bf16[152,3584]{1,0:T(8,128)(2,1)} %wg0.1), channel_id=1, source_target_pairs={{0,8},{8,0},{1,9},{9,1},{2,10},{10,2},{3,11},{11,3},{4,12},{12,4},... | collective-permute-start | bytes 3268616 | tf_op jit(solution)/shard_map/ppermute | solution.py:242
  42.1 2.4 %collective-permute-start.2 = (bf16[152,3584]{1,0:T(8,128)(2,1)}, bf16[152,3584]{1,0:T(8,128)(2,1)}, u32[]{:S(2)}, u32[]{:S(2)}) collective-permute-start(bf16[152,3584]{1,0:T(8,128)(2,1)} %wu0.1), channel_id=1, source_target_pairs={{0,8},{8,0},{1,9},{9,1},{2,10},{10,2},{3,11},{11,3},{4,12},{12,4},... | collective-permute-start | bytes 3268616 | tf_op jit(solution)/shard_map/ppermute | solution.py:242
  44.5 0.0 copy-done.2
  44.5 1.9 %collective-permute-start = (bf16[152,3584]{1,0:T(8,128)(2,1)S(1)}, bf16[152,3584]{1,0:T(8,128)(2,1)}, u32[]{:S(2)}, u32[]{:S(2)}) collective-permute-start(bf16[152,3584]{1,0:T(8,128)(2,1)S(1)} %copy-done.2), channel_id=1, source_target_pairs={{0,8},{8,0},{1,9},{9,1},{2,10},{10,2},{3,11},{11,3},{4,12},{12,4},... | collective-permute-start | bytes 3268616 | tf_op jit(solution)/shard_map/ppermute | solution.py:242
  46.4 2.4 %collective-permute-start.3 = (bf16[152,640]{1,0:T(8,128)(2,1)}, bf16[152,640]{1,0:T(8,128)(2,1)S(1)}, u32[]{:S(2)}, u32[]{:S(2)}) collective-permute-start(bf16[152,640]{1,0:T(8,128)(2,1)} %sg0.1), channel_id=1, source_target_pairs={{0,8},{8,0},{1,9},{9,1},{2,10},{10,2},{3,11},{11,3},{4,12},{12,4},... | collective-permute-start | bytes 583688 | tf_op jit(solution)/shard_map/ppermute | solution.py:242
  48.9 1.9 %collective-permute-start.4 = (bf16[152,640]{1,0:T(8,128)(2,1)}, bf16[152,640]{1,0:T(8,128)(2,1)S(1)}, u32[]{:S(2)}, u32[]{:S(2)}) collective-permute-start(bf16[152,640]{1,0:T(8,128)(2,1)} %su0.1), channel_id=1, source_target_pairs={{0,8},{8,0},{1,9},{9,1},{2,10},{10,2},{3,11},{11,3},{4,12},{12,4},... | collective-permute-start | bytes 583688 | tf_op jit(solution)/shard_map/ppermute | solution.py:242
  50.8 0.0 collective-permute-done.3.sg1
  50.8 0.0 copy-start.4
  50.8 1.6 %collective-permute-done.4.su1 = bf16[152,640]{1,0:T(8,128)(2,1)S(1)} collective-permute-done((bf16[152,640]{1,0:T(8,128)(2,1)}, bf16[152,640]{1,0:T(8,128)(2,1)S(1)}, u32[]{:S(2)}, u32[]{:S(2)}) %collective-permute-start.4) | collective-permute-done | bytes 194592 | tf_op jit(solution)/shard_map/ppermute | solution.py:242
  52.4 0.0 copy-start.5
  52.4 0.0 collective-permute-done.1.wg1
  52.4 0.0 copy-start.3
  52.4 0.0 collective-permute-done.2.wu1
  52.4 0.0 collective-permute-done.wd1
  52.4 0.0 copy-done.4
  52.4 0.6 copy-done.5
  53.1 0.5 copy-done.3
  53.5 7.8 %shard_map.84.w_hbm = bf16[1280,3584]{1,0:T(8,128)(2,1)} custom-call(bf16[152,3584]{1,0:T(8,128)(2,1)} %wd0.1, bf16[152,3584]{1,0:T(8,128)(2,1)} %collective-permute-done.wd1, bf16[152,3584]{1,0:T(8,128)(2,1)} %wg0.1, bf16[152,3584]{1,0:T(8,128)(2,1)} %copy-done.3, bf16[152,3584]{1,0:T(8,128)(2,1)} %wu0.1, bf16[152,3584]{1,0:T(8,128)(2,1)} %collective-permute-done.2.wu1, ...), custom_call_target="tpu_custom_call" | custom-call | flops 500000000 | bytes 16000000 | tf_op jit(solution)/shard_map/pallas_call | solution.py:268
  61.4 7.5 %all-to-all-done.1 = bf16[8,1120,128]{2,1,0:T(8,128)(2,1)S(1)} async-done(((bf16[8,1120,128]{2,1,0:T(8,128)(2,1)}), bf16[8,1120,128]{2,1,0:T(8,128)(2,1)S(1)}, u32[]{:S(2)}, u32[]{:S(2)}) %all-to-all-start.1) | async-done | bytes 2293792 | tf_op jit(solution)/shard_map/all_to_all | solution.py:247
  68.9 6.0 %shard_map.85 = bf16[8960,128]{1,0:T(8,128)(2,1)S(1)} custom-call(bf16[8960,128]{1,0:T(8,128)(2,1)S(1)} %bitcast.12, bf16[1280,3584]{1,0:T(8,128)(2,1)} %shard_map.84.w_hbm), custom_call_target="tpu_custom_call" | custom-call | flops 2300000000 | bytes 12000000 | tf_op jit(solution)/shard_map/pallas_call | solution.py:279
  74.9 32.0 %all_to_all.21 = bf16[8,1120,128]{2,1,0:T(8,128)(2,1)S(1)} all-to-all(bf16[8,1120,128]{2,1,0:T(8,128)(2,1)S(1)} %bitcast.13), channel_id=1, replica_groups=mesh['z'=8,'yh'=4,'core'=2,'x'=4,'yl'=2] {'x','yl'}, dimensions={0} | all-to-all | bytes 4587520 | tf_op jit(solution)/shard_map/all_to_all | solution.py:247
  106.9 0.0 copy-start.1
  106.9 0.9 shard_map.86
  107.8 19.3 %all_to_all.22 = bf16[32,40,128]{2,1,0:T(8,128)(2,1)S(1)} all-to-all(bf16[32,40,128]{2,1,0:T(8,128)(2,1)S(1)} %bitcast.18), channel_id=1, replica_groups=mesh['z'=8,'yh'=4,'core'=2,'x'=4,'yl'=2] {'z','yh'}, dimensions={0} | all-to-all | bytes 655360 | tf_op jit(solution)/shard_map/all_to_all | solution.py:247
  127.1 0.0 copy-done.1
  127.1 1.1 shard_map.87
Async XLA Ops:
  34.4 1.4 %copy-start = (bf16[8960,128]{1,0:T(8,128)(2,1)}, bf16[8960,128]{1,0:T(8,128)(2,1)S(1)}, u32[]{:S(2)}) copy-start(bf16[8960,128]{1,0:T(8,128)(2,1)S(1)} %shard_map.83) | copy-start | bytes 6881284
  35.7 8.8 %copy-start.2 = (bf16[152,3584]{1,0:T(8,128)(2,1)S(1)}, bf16[152,3584]{1,0:T(8,128)(2,1)}, u32[]{:S(2)}) copy-start(bf16[152,3584]{1,0:T(8,128)(2,1)} %wd0.1) | copy-start | bytes 3268612
  35.7 33.1 %all-to-all-start.1 = ((bf16[8,1120,128]{2,1,0:T(8,128)(2,1)}), bf16[8,1120,128]{2,1,0:T(8,128)(2,1)S(1)}, u32[]{:S(2)}, u32[]{:S(2)}) async-start(bf16[8,1120,128]{2,1,0:T(8,128)(2,1)} %bitcast.14), calls=%async_computation.1 | async-start | bytes 4587520 | tf_op jit(solution)/shard_map/all_to_all | solution.py:247
  40.2 12.2 %collective-permute-start.1 = (bf16[152,3584]{1,0:T(8,128)(2,1)}, bf16[152,3584]{1,0:T(8,128)(2,1)S(1)}, u32[]{:S(2)}, u32[]{:S(2)}) collective-permute-start(bf16[152,3584]{1,0:T(8,128)(2,1)} %wg0.1), channel_id=1, source_target_pairs={{0,8},{8,0},{1,9},{9,1},{2,10},{10,2},{3,11},{11,3},{4,12},{12,4},... | collective-permute-start | bytes 3268616 | tf_op jit(solution)/shard_map/ppermute | solution.py:242
  42.1 10.3 %collective-permute-start.2 = (bf16[152,3584]{1,0:T(8,128)(2,1)}, bf16[152,3584]{1,0:T(8,128)(2,1)}, u32[]{:S(2)}, u32[]{:S(2)}) collective-permute-start(bf16[152,3584]{1,0:T(8,128)(2,1)} %wu0.1), channel_id=1, source_target_pairs={{0,8},{8,0},{1,9},{9,1},{2,10},{10,2},{3,11},{11,3},{4,12},{12,4},... | collective-permute-start | bytes 3268616 | tf_op jit(solution)/shard_map/ppermute | solution.py:242
  44.5 7.9 %collective-permute-start = (bf16[152,3584]{1,0:T(8,128)(2,1)S(1)}, bf16[152,3584]{1,0:T(8,128)(2,1)}, u32[]{:S(2)}, u32[]{:S(2)}) collective-permute-start(bf16[152,3584]{1,0:T(8,128)(2,1)S(1)} %copy-done.2), channel_id=1, source_target_pairs={{0,8},{8,0},{1,9},{9,1},{2,10},{10,2},{3,11},{11,3},{4,12},{12,4},... | collective-permute-start | bytes 3268616 | tf_op jit(solution)/shard_map/ppermute | solution.py:242
  46.4 4.3 %collective-permute-start.3 = (bf16[152,640]{1,0:T(8,128)(2,1)}, bf16[152,640]{1,0:T(8,128)(2,1)S(1)}, u32[]{:S(2)}, u32[]{:S(2)}) collective-permute-start(bf16[152,640]{1,0:T(8,128)(2,1)} %sg0.1), channel_id=1, source_target_pairs={{0,8},{8,0},{1,9},{9,1},{2,10},{10,2},{3,11},{11,3},{4,12},{12,4},... | collective-permute-start | bytes 583688 | tf_op jit(solution)/shard_map/ppermute | solution.py:242
  48.9 3.5 %collective-permute-start.4 = (bf16[152,640]{1,0:T(8,128)(2,1)}, bf16[152,640]{1,0:T(8,128)(2,1)S(1)}, u32[]{:S(2)}, u32[]{:S(2)}) collective-permute-start(bf16[152,640]{1,0:T(8,128)(2,1)} %su0.1), channel_id=1, source_target_pairs={{0,8},{8,0},{1,9},{9,1},{2,10},{10,2},{3,11},{11,3},{4,12},{12,4},... | collective-permute-start | bytes 583688 | tf_op jit(solution)/shard_map/ppermute | solution.py:242
  50.8 1.6 %copy-start.4 = (bf16[152,640]{1,0:T(8,128)(2,1)}, bf16[152,640]{1,0:T(8,128)(2,1)S(1)}, u32[]{:S(2)}) copy-start(bf16[152,640]{1,0:T(8,128)(2,1)S(1)} %collective-permute-done.3.sg1) | copy-start | bytes 583684
  52.4 0.7 copy-start.5
  52.4 1.1 copy-start.3
  106.9 20.2 %copy-start.1 = (s32[2,128]{1,0:T(2,128)S(1)}, s32[2,128]{1,0:T(2,128)}, u32[]{:S(2)}) copy-start(s32[2,128]{1,0:T(2,128)} %get-tuple-element.8.tgt_ref) | copy-start | bytes 3076

commit v8 on v5

--- a/solution.py
+++ b/solution.py
@@ -100,10 +100,8 @@
     res = jnp.dot(moves, both, preferred_element_type=F32).astype(BF)
     for b in range(7):
         for g in range(2):
-            block = res[b * rows : (b + 1) * rows, g * 128 : (g + 1) * 128]
-            for t in range(TEN):
-                at = t * PIECE + b * HROWS + g * rows
-                out_ref[at : at + rows, :] = block
+            at = b * HROWS + g * rows
+            out_ref[at : at + rows, :] = res[b * rows : (b + 1) * rows, g * 128 : (g + 1) * 128]
 
 
 def stack_kernel(wd0, wd1, wg0, wg1, wu0, wu1, sg0, sg1, su0, su1, w_ref, sg_ref, su_ref, f_ref):
@@ -260,7 +258,8 @@
         limit=BIG,
     )(out_grad.T, gate_probs.T, expert_ids.T)
     got = exchange(packed, ("yh", "z"), EXP)
-    spread = call(sort_kernel, sds((TEN * PIECE, 128)), [VM], 10**9, 3 * 10**6)(got)
+    mine = call(sort_kernel, sds((PIECE, 128)), [VM], 10**9, 10**6)(got)
+    spread = jnp.broadcast_to(mine[None], (TEN, PIECE, 128)).reshape(TEN * PIECE, 128)
     pieces = exchange(spread, ("yl", "x"), TEN)
 
     operands = []

time: 129 us -> 129 us (level)
    broadcast_in_dim x0 -> x1, local copies, waits for them, and re-layouts: none -> 1.67 us  [shards(): jnp.broadcast_to(mine[None], (TEN, PIECE, 128)).reshape(TEN * PIECE, 128)]
    unnamed x12 -> x10, local copies, waits for them, and re-layouts: 2.47 us -> 1.12 us
where the time goes in v8:
time: 129 us; the launch traced here: 127 us
  blocking collectives  82 us (64%)
  Pallas kernels  18.9 us (15%)
  starting transfers between devices  18.2 us (14%)
  waiting for transfers between devices  4.7 us (4%)
  local copies, waits for them, and re-layouts  2.79 us (2%)
    all_to_all x3, blocking collectives, exchange(): lax.all_to_all(blocks, axes, split_axis=0, concat_axis=0, tiled=True)  82 us
    ppermute x5, starting transfers between devices, swap_core(): return lax.ppermute(a, 'core', [(0, 1), (1, 0)])  14 us
    pallas_call x1, Pallas kernels, shards(): call(stack_kernel, sds((6 * FPAD + ROWS, D)), [block] * 6 + [saved] * 4,...  7.88 us
    pallas_call x1, Pallas kernels, shards(): call(main_kernel, sds((TEN * PIECE, 128)), [VM, AN], 23 * 10 ** 8, 12 * 1...  6.03 us
    all_to_all x1, starting transfers between devices, exchange(): lax.all_to_all(blocks, axes, split_axis=0, concat_axis=0, tiled=True)  4.15 us
    all_to_all x1, waiting for transfers between devices, exchange(): lax.all_to_all(blocks, axes, split_axis=0, concat_axis=0, tiled=True)  3.45 us
    pallas_call x1, Pallas kernels, shards(): call(pack_kernel, [sds((EXP * BLK, 128)), sds((2, TOK), jnp.int32)], [VM,...  2.62 us
  transfers between devices with their start and end apart: 6, of which 2 were waited for; matrix products, arithmetic and copies ran while one was open for 0% of the time, Pallas kernels for 6%

profile of v8, /device:TPU:1, one launch (start us, length us, event | category | flops | bytes accessed | tf_op | source)
XLA Modules:
  0.0 126.6 jit_solution(5024126926855352892)
XLA Ops:
  0.0 2.6 %shard_map.82 = (bf16[1280,128]{1,0:T(8,128)(2,1)}, s32[2,128]{1,0:T(2,128)}) custom-call(bf16[448,128]{1,0:T(8,128)(2,1)} %bitcast.18, f32[2,128]{1,0:T(2,128)} %bitcast.19, s32[2,128]{1,0:T(2,128)} %bitcast.20), custom_call_target="tpu_custom_call" | custom-call | flops 1000000000 | bytes 1000000 | tf_op jit(solution)/shard_map/pallas_call | solution.py:252
  2.6 29.8 %all_to_all.20 = bf16[32,40,128]{2,1,0:T(8,128)(2,1)S(1)} all-to-all(bf16[32,40,128]{2,1,0:T(8,128)(2,1)} %bitcast.17), channel_id=1, replica_groups=mesh['z'=8,'yh'=4,'core'=2,'x'=4,'yl'=2] {'yh','z'}, dimensions={0} | all-to-all | bytes 655360 | tf_op jit(solution)/shard_map/all_to_all | solution.py:248
  32.4 0.4 shard_map.83
  32.8 1.7 %broadcast_in_dim.2 = bf16[8,1120,128]{2,1,0:T(8,128)(2,1)} broadcast(bf16[1120,128]{1,0:T(8,128)(2,1)S(1)} %shard_map.83), dimensions={1,2} | broadcast | bytes 2580480 | tf_op jit(solution)/shard_map/broadcast_in_dim | solution.py:262
  34.5 0.0 copy-start.1
  34.5 4.1 %all-to-all-start.1 = ((bf16[8,1120,128]{2,1,0:T(8,128)(2,1)}), bf16[8,1120,128]{2,1,0:T(8,128)(2,1)S(1)}, u32[]{:S(2)}, u32[]{:S(2)}) async-start(bf16[8,1120,128]{2,1,0:T(8,128)(2,1)} %broadcast_in_dim.2), calls=%async_computation.1 | async-start | bytes 4587520 | tf_op jit(solution)/shard_map/all_to_all | solution.py:248
  38.6 5.4 %collective-permute-start.1 = (bf16[152,3584]{1,0:T(8,128)(2,1)}, bf16[152,3584]{1,0:T(8,128)(2,1)S(1)}, u32[]{:S(2)}, u32[]{:S(2)}) collective-permute-start(bf16[152,3584]{1,0:T(8,128)(2,1)} %wg0.1), channel_id=1, source_target_pairs={{0,8},{8,0},{1,9},{9,1},{2,10},{10,2},{3,11},{11,3},{4,12},{12,4},... | collective-permute-start | bytes 3268616 | tf_op jit(solution)/shard_map/ppermute | solution.py:243
  44.0 1.9 %collective-permute-start.2 = (bf16[152,3584]{1,0:T(8,128)(2,1)}, bf16[152,3584]{1,0:T(8,128)(2,1)}, u32[]{:S(2)}, u32[]{:S(2)}) collective-permute-start(bf16[152,3584]{1,0:T(8,128)(2,1)} %wu0.1), channel_id=1, source_target_pairs={{0,8},{8,0},{1,9},{9,1},{2,10},{10,2},{3,11},{11,3},{4,12},{12,4},... | collective-permute-start | bytes 3268616 | tf_op jit(solution)/shard_map/ppermute | solution.py:243
  45.9 0.0 copy-done.1
  45.9 2.4 %collective-permute-start = (bf16[152,3584]{1,0:T(8,128)(2,1)S(1)}, bf16[152,3584]{1,0:T(8,128)(2,1)}, u32[]{:S(2)}, u32[]{:S(2)}) collective-permute-start(bf16[152,3584]{1,0:T(8,128)(2,1)S(1)} %copy-done.1), channel_id=1, source_target_pairs={{0,8},{8,0},{1,9},{9,1},{2,10},{10,2},{3,11},{11,3},{4,12},{12,4},... | collective-permute-start | bytes 3268616 | tf_op jit(solution)/shard_map/ppermute | solution.py:243
  48.3 1.9 %collective-permute-start.3 = (bf16[152,640]{1,0:T(8,128)(2,1)}, bf16[152,640]{1,0:T(8,128)(2,1)S(1)}, u32[]{:S(2)}, u32[]{:S(2)}) collective-permute-start(bf16[152,640]{1,0:T(8,128)(2,1)} %sg0.1), channel_id=1, source_target_pairs={{0,8},{8,0},{1,9},{9,1},{2,10},{10,2},{3,11},{11,3},{4,12},{12,4},... | collective-permute-start | bytes 583688 | tf_op jit(solution)/shard_map/ppermute | solution.py:243
  50.3 2.4 %collective-permute-start.4 = (bf16[152,640]{1,0:T(8,128)(2,1)}, bf16[152,640]{1,0:T(8,128)(2,1)S(1)}, u32[]{:S(2)}, u32[]{:S(2)}) collective-permute-start(bf16[152,640]{1,0:T(8,128)(2,1)} %su0.1), channel_id=1, source_target_pairs={{0,8},{8,0},{1,9},{9,1},{2,10},{10,2},{3,11},{11,3},{4,12},{12,4},... | collective-permute-start | bytes 583688 | tf_op jit(solution)/shard_map/ppermute | solution.py:243
  52.7 0.0 collective-permute-done.3.sg1
  52.7 0.0 copy-start.3
  52.7 1.2 collective-permute-done.4.su1
  54.0 0.0 copy-start.4
  54.0 0.0 collective-permute-done.1.wg1
  54.0 0.0 copy-start.2
  54.0 0.0 collective-permute-done.2.wu1
  54.0 0.0 collective-permute-done.wd1
  54.0 0.0 copy-done.3
  54.0 0.6 copy-done.4
  54.6 0.5 copy-done.2
  55.1 7.9 %shard_map.84.w_hbm = bf16[1280,3584]{1,0:T(8,128)(2,1)} custom-call(bf16[152,3584]{1,0:T(8,128)(2,1)} %wd0.1, bf16[152,3584]{1,0:T(8,128)(2,1)} %collective-permute-done.wd1, bf16[152,3584]{1,0:T(8,128)(2,1)} %wg0.1, bf16[152,3584]{1,0:T(8,128)(2,1)} %copy-done.2, bf16[152,3584]{1,0:T(8,128)(2,1)} %wu0.1, bf16[152,3584]{1,0:T(8,128)(2,1)} %collective-permute-done.2.wu1, ...), custom_call_target="tpu_custom_call" | custom-call | flops 500000000 | bytes 16000000 | tf_op jit(solution)/shard_map/pallas_call | solution.py:270
  63.0 3.5 %all-to-all-done.1 = bf16[8,1120,128]{2,1,0:T(8,128)(2,1)S(1)} async-done(((bf16[8,1120,128]{2,1,0:T(8,128)(2,1)}), bf16[8,1120,128]{2,1,0:T(8,128)(2,1)S(1)}, u32[]{:S(2)}, u32[]{:S(2)}) %all-to-all-start.1) | async-done | bytes 2293792 | tf_op jit(solution)/shard_map/all_to_all | solution.py:248
  66.4 6.0 %shard_map.85 = bf16[8960,128]{1,0:T(8,128)(2,1)S(1)} custom-call(bf16[8960,128]{1,0:T(8,128)(2,1)S(1)} %bitcast.11, bf16[1280,3584]{1,0:T(8,128)(2,1)} %shard_map.84.w_hbm), custom_call_target="tpu_custom_call" | custom-call | flops 2300000000 | bytes 12000000 | tf_op jit(solution)/shard_map/pallas_call | solution.py:281
  72.5 32.6 %all_to_all.21 = bf16[8,1120,128]{2,1,0:T(8,128)(2,1)S(1)} all-to-all(bf16[8,1120,128]{2,1,0:T(8,128)(2,1)S(1)} %bitcast.12), channel_id=1, replica_groups=mesh['z'=8,'yh'=4,'core'=2,'x'=4,'yl'=2] {'x','yl'}, dimensions={0} | all-to-all | bytes 4587520 | tf_op jit(solution)/shard_map/all_to_all | solution.py:248
  105.1 0.0 copy-start
  105.1 0.9 shard_map.86
  105.9 19.6 %all_to_all.22 = bf16[32,40,128]{2,1,0:T(8,128)(2,1)S(1)} all-to-all(bf16[32,40,128]{2,1,0:T(8,128)(2,1)S(1)} %bitcast.16), channel_id=1, replica_groups=mesh['z'=8,'yh'=4,'core'=2,'x'=4,'yl'=2] {'yh','z'}, dimensions={0} | all-to-all | bytes 655360 | tf_op jit(solution)/shard_map/all_to_all | solution.py:248
  125.5 0.0 copy-done
  125.5 1.1 shard_map.87
Async XLA Ops:
  34.5 11.4 %copy-start.1 = (bf16[152,3584]{1,0:T(8,128)(2,1)S(1)}, bf16[152,3584]{1,0:T(8,128)(2,1)}, u32[]{:S(2)}) copy-start(bf16[152,3584]{1,0:T(8,128)(2,1)} %wd0.1) | copy-start | bytes 3268612
  34.5 31.9 %all-to-all-start.1 = ((bf16[8,1120,128]{2,1,0:T(8,128)(2,1)}), bf16[8,1120,128]{2,1,0:T(8,128)(2,1)S(1)}, u32[]{:S(2)}, u32[]{:S(2)}) async-start(bf16[8,1120,128]{2,1,0:T(8,128)(2,1)} %broadcast_in_dim.2), calls=%async_computation.1 | async-start | bytes 4587520 | tf_op jit(solution)/shard_map/all_to_all | solution.py:248
  38.6 15.3 %collective-permute-start.1 = (bf16[152,3584]{1,0:T(8,128)(2,1)}, bf16[152,3584]{1,0:T(8,128)(2,1)S(1)}, u32[]{:S(2)}, u32[]{:S(2)}) collective-permute-start(bf16[152,3584]{1,0:T(8,128)(2,1)} %wg0.1), channel_id=1, source_target_pairs={{0,8},{8,0},{1,9},{9,1},{2,10},{10,2},{3,11},{11,3},{4,12},{12,4},... | collective-permute-start | bytes 3268616 | tf_op jit(solution)/shard_map/ppermute | solution.py:243
  44.0 10.0 %collective-permute-start.2 = (bf16[152,3584]{1,0:T(8,128)(2,1)}, bf16[152,3584]{1,0:T(8,128)(2,1)}, u32[]{:S(2)}, u32[]{:S(2)}) collective-permute-start(bf16[152,3584]{1,0:T(8,128)(2,1)} %wu0.1), channel_id=1, source_target_pairs={{0,8},{8,0},{1,9},{9,1},{2,10},{10,2},{3,11},{11,3},{4,12},{12,4},... | collective-permute-start | bytes 3268616 | tf_op jit(solution)/shard_map/ppermute | solution.py:243
  45.9 8.0 %collective-permute-start = (bf16[152,3584]{1,0:T(8,128)(2,1)S(1)}, bf16[152,3584]{1,0:T(8,128)(2,1)}, u32[]{:S(2)}, u32[]{:S(2)}) collective-permute-start(bf16[152,3584]{1,0:T(8,128)(2,1)S(1)} %copy-done.1), channel_id=1, source_target_pairs={{0,8},{8,0},{1,9},{9,1},{2,10},{10,2},{3,11},{11,3},{4,12},{12,4},... | collective-permute-start | bytes 3268616 | tf_op jit(solution)/shard_map/ppermute | solution.py:243
  48.3 4.3 %collective-permute-start.3 = (bf16[152,640]{1,0:T(8,128)(2,1)}, bf16[152,640]{1,0:T(8,128)(2,1)S(1)}, u32[]{:S(2)}, u32[]{:S(2)}) collective-permute-start(bf16[152,640]{1,0:T(8,128)(2,1)} %sg0.1), channel_id=1, source_target_pairs={{0,8},{8,0},{1,9},{9,1},{2,10},{10,2},{3,11},{11,3},{4,12},{12,4},... | collective-permute-start | bytes 583688 | tf_op jit(solution)/shard_map/ppermute | solution.py:243
  50.3 3.7 %collective-permute-start.4 = (bf16[152,640]{1,0:T(8,128)(2,1)}, bf16[152,640]{1,0:T(8,128)(2,1)S(1)}, u32[]{:S(2)}, u32[]{:S(2)}) collective-permute-start(bf16[152,640]{1,0:T(8,128)(2,1)} %su0.1), channel_id=1, source_target_pairs={{0,8},{8,0},{1,9},{9,1},{2,10},{10,2},{3,11},{11,3},{4,12},{12,4},... | collective-permute-start | bytes 583688 | tf_op jit(solution)/shard_map/ppermute | solution.py:243
  52.7 1.3 %copy-start.3 = (bf16[152,640]{1,0:T(8,128)(2,1)}, bf16[152,640]{1,0:T(8,128)(2,1)S(1)}, u32[]{:S(2)}) copy-start(bf16[152,640]{1,0:T(8,128)(2,1)S(1)} %collective-permute-done.3.sg1) | copy-start | bytes 583684
  54.0 0.7 copy-start.4
  54.0 1.1 copy-start.2
  105.1 20.4 %copy-start = (s32[2,128]{1,0:T(2,128)S(1)}, s32[2,128]{1,0:T(2,128)}, u32[]{:S(2)}) copy-start(s32[2,128]{1,0:T(2,128)} %get-tuple-element.8.tgt_ref) | copy-start | bytes 3076
